TPU v7x, 256 devices: a whole 4x4x8 slice. The times are simulated.
256 devices in a mesh: dp: 32 (over z, y_lo, core), seq: 8 (over y_hi, x).
Axes of the slice: x: 4, y: 4 (y_hi: 2, y_lo: 2; y = y_hi * 2 + y_lo), z: 8, core: 2. Of those that a mesh axis runs over, the one named last changes fastest.
Arguments:
- tokens: bfloat16 [65536, 1024], P(('dp', 'seq')), may hold values from -40 to 40
- lengths: int32 [32, 4], P('dp'), may hold values from 1 to 1024, 2048 in all within a row
- in_weight: bfloat16 [1024, 4096], P(('dp', 'seq')), may hold values from -0.1875 to 0.1875
- out_weight: bfloat16 [1024, 1024], P(('dp', 'seq')), may hold values from -0.1875 to 0.1875
- cotangent: bfloat16 [65536, 1024], P(('dp', 'seq')), may hold values from -6 to 6
Outputs:
- layer_out: bfloat16 [65536, 1024], P(('dp', 'seq'))
- tokens_grad: bfloat16 [65536, 1024], P(('dp', 'seq'))
- in_weight_grad: float32 [1024, 4096], P(('dp', 'seq'))
- out_weight_grad: float32 [1024, 1024], P(('dp', 'seq'))
Inputs may be any that keep to these rules, and one draw needn't show every extreme that they name: Row g holds the lengths of the 4 histories of group g, which fill its 2048 positions; the longest of every row is exactly 1024.
All inputs are finite; a program needn't handle non-finite values.
Results may differ from a plain program's by a relative error of at most 0.034.
Values may be sent and summed in bfloat16 or wider, within the bound.
A program may use at most 128 MiB of HBM per device.

v0:
```python
import jax
import jax.numpy as jnp
from jax import lax
from jax.sharding import PartitionSpec as P

D = 1024
H = 8


epsilon = 1e-05


def normalize(values):
    centre = values - jnp.mean(values, axis=-1, keepdims=True)
    inverse = lax.rsqrt(jnp.mean(centre * centre, axis=-1, keepdims=True) + epsilon)
    return (centre * inverse, inverse)


def norm_back(upstream, normed, inverse):
    first = jnp.mean(upstream, axis=-1, keepdims=True)
    second = jnp.mean(upstream * normed, axis=-1, keepdims=True)
    return inverse * (upstream - first - normed * second)


def to_heads(stacked):
    return lax.all_to_all(stacked, "seq", split_axis=2, concat_axis=0, tiled=True)


def to_tokens(stacked):
    return lax.all_to_all(stacked, "seq", split_axis=0, concat_axis=2, tiled=True)


def layout_of(heads):
    head_size = D // H
    length_all = heads.shape[0]
    per_device = heads.shape[2] // head_size
    block_rows = min(512, length_all)
    return (head_size, length_all, per_device, block_rows)


def attend(heads, seg_ids):
    head_size, length_all, per_device, block_rows = layout_of(heads)
    columns = heads.shape[2]
    values = heads[:, 0].reshape(length_all, per_device, head_size)
    queries = heads[:, 1].reshape(length_all, per_device, head_size)
    keys = heads[:, 2].reshape(length_all, per_device, head_size)
    position = jnp.arange(length_all, dtype=jnp.int32)
    factor = head_size ** (-0.5)

    def one_query(number):
        q_start = number * block_rows
        query_rows = lax.dynamic_slice_in_dim(queries, q_start, block_rows, 0)
        seg_query = lax.dynamic_slice_in_dim(seg_ids, q_start, block_rows, 0)
        pos_query = lax.dynamic_slice_in_dim(position, q_start, block_rows, 0)

        def add_key(inner_step, summed):
            k_start = inner_step * block_rows
            key_rows = lax.dynamic_slice_in_dim(keys, k_start, block_rows, 0)
            value_rows = lax.dynamic_slice_in_dim(values, k_start, block_rows, 0)
            seg_key = lax.dynamic_slice_in_dim(seg_ids, k_start, block_rows, 0)
            pos_key = lax.dynamic_slice_in_dim(position, k_start, block_rows, 0)

            def compute(running):
                scores = (
                    jnp.einsum(
                        "qhd,khd->hqk", query_rows, key_rows, preferred_element_type=jnp.float32
                    )
                    * factor
                )
                allowed = (seg_query[:, None] == seg_key[None, :]) & (
                    pos_key[None, :] <= pos_query[:, None]
                )
                weights = jnp.where(allowed[None], jax.nn.silu(scores), 0.0).astype(jnp.bfloat16)
                return running + jnp.einsum(
                    "hqk,khd->qhd", weights, value_rows, preferred_element_type=jnp.float32
                )

            result = compute(summed)
            return result

        summed = lax.fori_loop(
            0, number + 1, add_key, jnp.zeros((block_rows, per_device, head_size), jnp.float32)
        )
        return summed.astype(jnp.bfloat16).reshape(block_rows, columns)

    outputs = lax.map(one_query, jnp.arange(length_all // block_rows, dtype=jnp.int32))
    return outputs.reshape(length_all, 1, columns)


def attend_back(heads, seg_ids, d_heads):
    head_size, length_all, per_device, block_rows = layout_of(heads)
    columns = heads.shape[2]
    values = heads[:, 0].reshape(length_all, per_device, head_size)
    queries = heads[:, 1].reshape(length_all, per_device, head_size)
    keys = heads[:, 2].reshape(length_all, per_device, head_size)
    position = jnp.arange(length_all, dtype=jnp.int32)
    factor = head_size ** (-0.5)
    zeros_all = jnp.zeros((length_all, per_device, head_size), jnp.float32)

    def one_query(number, carried):
        grad_keys, grad_values, grad_queries = carried
        q_start = number * block_rows
        query_rows = lax.dynamic_slice_in_dim(queries, q_start, block_rows, 0)
        d_query = lax.dynamic_slice_in_dim(d_heads, q_start, block_rows, 0)
        seg_query = lax.dynamic_slice_in_dim(seg_ids, q_start, block_rows, 0)
        pos_query = lax.dynamic_slice_in_dim(position, q_start, block_rows, 0)

        def add_key(inner_step, state):
            k_start = inner_step * block_rows
            key_rows = lax.dynamic_slice_in_dim(keys, k_start, block_rows, 0)
            value_rows = lax.dynamic_slice_in_dim(values, k_start, block_rows, 0)
            seg_key = lax.dynamic_slice_in_dim(seg_ids, k_start, block_rows, 0)
            pos_key = lax.dynamic_slice_in_dim(position, k_start, block_rows, 0)

            def compute(running):
                query_acc, key_grads, value_grads = running
                scores = (
                    jnp.einsum(
                        "qhd,khd->hqk", query_rows, key_rows, preferred_element_type=jnp.float32
                    )
                    * factor
                )
                allowed = (
                    (seg_query[:, None] == seg_key[None, :])
                    & (pos_key[None, :] <= pos_query[:, None])
                )[None]
                sigma = jax.nn.sigmoid(scores)
                weights = jnp.where(allowed, jax.nn.silu(scores), 0.0).astype(jnp.bfloat16)
                d_weights = jnp.einsum(
                    "qhd,khd->hqk", d_query, value_rows, preferred_element_type=jnp.float32
                )
                d_scores = (
                    jnp.where(allowed, d_weights * sigma * (1.0 + scores * (1.0 - sigma)), 0.0)
                    * factor
                ).astype(jnp.bfloat16)
                query_acc = query_acc + jnp.einsum(
                    "hqk,khd->qhd", d_scores, key_rows, preferred_element_type=jnp.float32
                )
                key_part = jnp.einsum(
                    "hqk,qhd->khd", d_scores, query_rows, preferred_element_type=jnp.float32
                )
                value_part = jnp.einsum(
                    "hqk,qhd->khd", weights, d_query, preferred_element_type=jnp.float32
                )
                key_old = lax.dynamic_slice_in_dim(key_grads, k_start, block_rows, 0)
                value_old = lax.dynamic_slice_in_dim(value_grads, k_start, block_rows, 0)
                key_grads = lax.dynamic_update_slice_in_dim(
                    key_grads, key_old + key_part, k_start, 0
                )
                value_grads = lax.dynamic_update_slice_in_dim(
                    value_grads, value_old + value_part, k_start, 0
                )
                return (query_acc, key_grads, value_grads)

            result = compute(state)
            return result

        start_state = (
            jnp.zeros((block_rows, per_device, head_size), jnp.float32),
            grad_keys,
            grad_values,
        )
        query_acc, grad_keys, grad_values = lax.fori_loop(0, number + 1, add_key, start_state)
        grad_queries = lax.dynamic_update_slice_in_dim(grad_queries, query_acc, q_start, 0)
        return (grad_keys, grad_values, grad_queries)

    grad_keys, grad_values, grad_queries = lax.fori_loop(
        0, length_all // block_rows, one_query, (zeros_all, zeros_all, zeros_all)
    )
    stacked = jnp.stack([grad_values, grad_queries, grad_keys], axis=1)
    return stacked.astype(jnp.bfloat16).reshape(length_all, 3, columns)


def local(tokens, lengths, in_weight, out_weight, cotangent):
    rows_here, width = tokens.shape
    full_in, full_out = (
        lax.all_gather(in_weight, ("dp", "seq"), axis=0, tiled=True),
        lax.all_gather(out_weight, ("dp", "seq"), axis=0, tiled=True),
    )
    token_f = tokens.astype(jnp.float32)
    normed_in, rstd_in = normalize(token_f)
    normed_bf = normed_in.astype(jnp.bfloat16)
    hidden = jnp.dot(normed_bf, full_in, preferred_element_type=jnp.float32)
    gated = jax.nn.silu(hidden).astype(jnp.bfloat16)
    upper = gated[:, :width].astype(jnp.float32)
    trio = gated[:, width:].reshape(rows_here, 3, width)
    heads = to_heads(trio)
    length_all = heads.shape[0]
    position = jnp.arange(length_all, dtype=jnp.int32)
    ends = jnp.cumsum(lengths[0])
    seg_ids = jnp.sum((position[:, None] >= ends[None, :-1]).astype(jnp.int32), axis=1)
    attn_heads = attend(heads, seg_ids)
    attn = to_tokens(attn_heads).reshape(rows_here, width)
    normed_out, rstd_out = normalize(attn.astype(jnp.float32))
    mixed = (normed_out * upper).astype(jnp.bfloat16)
    layer_out = (jnp.dot(mixed, full_out, preferred_element_type=jnp.float32) + token_f).astype(
        jnp.bfloat16
    )
    contract_cols = (((1,), (1,)), ((), ()))
    contract_rows = (((0,), (0,)), ((), ()))
    d_mixed = lax.dot_general(
        cotangent, full_out, contract_cols, preferred_element_type=jnp.float32
    )
    d_attn = norm_back(d_mixed * upper, normed_out, rstd_out).astype(jnp.bfloat16)
    d_heads = to_heads(d_attn.reshape(rows_here, 1, width))
    grad_heads = attend_back(heads, seg_ids, d_heads)
    grad_trio = to_tokens(grad_heads).reshape(rows_here, 3 * width)
    d_gated = jnp.concatenate([d_mixed * normed_out, grad_trio.astype(jnp.float32)], axis=1)
    sigma = jax.nn.sigmoid(hidden)
    d_hidden = (d_gated * sigma * (1.0 + hidden * (1.0 - sigma))).astype(jnp.bfloat16)
    d_normed = lax.dot_general(d_hidden, full_in, contract_cols, preferred_element_type=jnp.float32)
    tokens_grad = (norm_back(d_normed, normed_in, rstd_in) + cotangent.astype(jnp.float32)).astype(
        jnp.bfloat16
    )
    in_partial = lax.dot_general(
        normed_bf, d_hidden, contract_rows, preferred_element_type=jnp.float32
    )
    out_partial = lax.dot_general(
        mixed, cotangent, contract_rows, preferred_element_type=jnp.float32
    )
    group_in, group_out = (
        lax.psum_scatter(
            in_partial.astype(jnp.bfloat16), "dp", scatter_dimension=0, tiled=True
        ).astype(jnp.float32),
        lax.psum_scatter(
            out_partial.astype(jnp.bfloat16), "dp", scatter_dimension=0, tiled=True
        ).astype(jnp.float32),
    )
    in_weight_grad, out_weight_grad = (
        lax.psum_scatter(
            group_in.astype(jnp.bfloat16), "seq", scatter_dimension=0, tiled=True
        ).astype(jnp.float32),
        lax.psum_scatter(
            group_out.astype(jnp.bfloat16), "seq", scatter_dimension=0, tiled=True
        ).astype(jnp.float32),
    )
    return (layer_out, tokens_grad, in_weight_grad, out_weight_grad)


def solution(mesh):
    return jax.shard_map(
        local,
        mesh=mesh,
        in_specs=(
            P(("dp", "seq"), None),
            P("dp", None),
            P(("dp", "seq"), None),
            P(("dp", "seq"), None),
            P(("dp", "seq"), None),
        ),
        out_specs=(
            P(("dp", "seq"), None),
            P(("dp", "seq"), None),
            P(("dp", "seq"), None),
            P(("dp", "seq"), None),
        ),
        check_vma=False,
    )
```

profile of v0, /device:TPU:1, one launch (start us, length us, event | category | flops | bytes accessed | tf_op | source)
XLA Modules:
  0.0 1942.7 jit_solution(9120413505294775914)
XLA Ops:
  10.5 721.0 %all-gather.5.cloned.1.call-done = bf16[256,4,4096]{2,1,0:T(4,128)(2,1)} async-done(((bf16[1,4,4096]{2,1,0:T(4,128)(2,1)}), bf16[256,4,4096]{2,1,0:T(4,128)(2,1)}) %all-gather.5.cloned.1.call-update) | async-done | bytes 8388624 | tf_op jit(solution)/shard_map/all_gather | solution.py:177
  731.5 12.6 reshape.191
  744.0 7.9 multiply_convert_fusion
  756.7 3.6 all-to-all-start
  761.4 27.4 %all-to-all-done = bf16[256,3,1024]{0,1,2:T(4,128)(2,1)S(1)} async-done(((bf16[256,3,1024]{0,1,2:T(4,128)(2,1)}), bf16[256,3,1024]{0,1,2:T(4,128)(2,1)S(1)}, u32[]{:S(2)}, u32[]{:S(2)}) %all-to-all-start) | async-done | bytes 1572896 | tf_op jit(solution)/shard_map/all_to_all | solution.py:26
  793.3 32.1 %while.72 = (s32[]{:T(128)}, bf16[4,512,128]{2,1,0:T(8,128)(2,1)S(1)}, s32[4]{0:T(128)S(1)}, bf16[2048,1,128]{2,0,1:T(8,128)(2,1)}, s32[2048]{0:T(1024)S(1)}, /*...) while((s32[]{:T(128)}, ...), condition=%wide.region_7.8_spmd.clone, body=%wide.region_4.7_spmd.clone.sunk | while | flops 136970240 | bytes 2385466 | solution.py:86
  801.6 3.8 while.75
  808.7 5.7 while.75
  817.7 7.5 while.75
  827.9 5.3 all-to-all-start.1
  833.2 629.0 %all-gather.7.cloned.1.call-done = bf16[256,4,1024]{2,1,0:T(4,128)(2,1)} async-done(((bf16[1,4,1024]{2,1,0:T(4,128)(2,1)}), bf16[256,4,1024]{2,1,0:T(4,128)(2,1)}) %all-gather.7.cloned.1.call-update) | async-done | bytes 2097168 | tf_op jit(solution)/shard_map/all_gather | solution.py:178
  1462.3 4.0 reshape.193
  1474.3 3.8 reduce.7
  1479.1 3.5 all-to-all-start.2
  1482.7 3.4 convolution_convert_fusion.1
  1486.3 7.9 all-to-all-done.2
  1499.6 149.4 %while.74 = (s32[]{:T(128)}, f32[2048,1,128]{2,0,1:T(8,128)}, f32[2048,1,128]{2,0,1:T(8,128)}, bf16[2048,1,128]{0,2,1:T(8,128)(2,1)}, bf16[2048,1,128]{2,0,1:T(8...) while((s32[]{:T(128)}, f32[2048,1,128]{2,0,1:T(8,128)}, ...), condition=%wide.region_16.17_spmd.clone, body=%wide.region_13.16_spmd.clone.sunk | while | flops 342032384 | bytes 19038880 | solution.py:167
  1503.9 12.5 while.76
  1522.4 25.1 %while.76 = (s32[]{:T(128)}, f32[512,1,128]{0,2,1:T(8,128)}, f32[2048,1,128]{2,0,1:T(8,128)}, f32[2048,1,128]{2,0,1:T(8,128)}, s32[]{:T(128)}, /*index=5*/bf16[2...) while((s32[]{:T(128)}, f32[512,1,128]{0,2,1:T(8,128)}, ...), condition=%wide.region_15.15_spmd, body=%wide.region_14.14_spmd.sunk | while | flops 342032384 | bytes 17719584 | solution.py:163
  1553.5 37.7 %while.76 = (s32[]{:T(128)}, f32[512,1,128]{0,2,1:T(8,128)}, f32[2048,1,128]{2,0,1:T(8,128)}, f32[2048,1,128]{2,0,1:T(8,128)}, s32[]{:T(128)}, /*index=5*/bf16[2...) while((s32[]{:T(128)}, f32[512,1,128]{0,2,1:T(8,128)}, ...), condition=%wide.region_15.15_spmd, body=%wide.region_14.14_spmd.sunk | while | flops 342032384 | bytes 17719584 | solution.py:163
  1583.4 2.7 fusion.115
  1597.1 50.2 %while.76 = (s32[]{:T(128)}, f32[512,1,128]{0,2,1:T(8,128)}, f32[2048,1,128]{2,0,1:T(8,128)}, f32[2048,1,128]{2,0,1:T(8,128)}, s32[]{:T(128)}, /*index=5*/bf16[2...) while((s32[]{:T(128)}, f32[512,1,128]{0,2,1:T(8,128)}, ...), condition=%wide.region_15.15_spmd, body=%wide.region_14.14_spmd.sunk | while | flops 342032384 | bytes 17719584 | solution.py:163
  1627.1 2.7 fusion.115
  1652.7 8.1 copy.104
  1660.9 8.3 copy.102
  1669.2 3.6 pad_maximum_fusion
  1672.8 30.3 %all_to_all.54 = bf16[2048,3,128]{2,1,0:T(4,128)(2,1)S(1)} all-to-all(bf16[2048,3,128]{2,1,0:T(4,128)(2,1)S(1)} %pad_maximum_fusion), channel_id=1, replica_groups=mesh['dp'=32,'seq'=8] {'seq'}, dimensions={0} | all-to-all | bytes 3145728 | tf_op jit(solution)/shard_map/all_to_all | solution.py:30
  1710.3 5.7 convolution_convert_fusion
  1718.0 3.5 fusion.53
  1721.5 5.9 fusion.78
  1727.5 116.7 %reduce-scatter.3.cloned.1.call-done = bf16[32,4096]{1,0:T(8,128)(2,1)} async-done(((bf16[1024,4096]{1,0:T(8,128)(2,1)}), bf16[32,4096]{1,0:T(8,128)(2,1)}) %reduce-scatter.3.cloned.1.call-update) | async-done | bytes 262160 | tf_op jit(solution)/shard_map/reduce_scatter | solution.py:222
  1845.5 87.6 %all-reduce.5.cloned.1.call-done = (bf16[32,4096]{1,0:T(8,128)(2,1)}, bf16[32,1024]{1,0:T(8,128)(2,1)}) async-done(((bf16[32,4096]{1,0:T(8,128)(2,1)}, bf16[32,1024]{1,0:T(8,128)(2,1)}), (bf16[32,4096]{1,0:T(8,128)(2,1)}, bf16[32,1024]{1,0:T(8,128)(2,1)})) %all-reduce.5.cloned.1.call-update) | async-done | bytes 327696
  (341 shorter events, 218.1 us)
Async XLA Ops:
  7.2 724.3 %all-gather.5.cloned.1.call-start = ((), (), s32[]{:S(2)}) async-start(), calls=%async_computation.8 | async-start | bytes 8421376 | tf_op jit(solution)/shard_map/all_gather | solution.py:177
  9.1 734.9 %copy-start.15 = (f32[256]{0:T(256)}, f32[256]{0:T(256)S(1)}, u32[]{:S(2)}) copy-start(f32[256]{0:T(256)S(1)} %broadcast_multiply_fusion.5) | copy-start | bytes 3076
  10.4 733.6 %copy-start.17 = (f32[256]{0:T(256)}, f32[256]{0:T(256)S(1)}, u32[]{:S(2)}) copy-start(f32[256]{0:T(256)S(1)} %add_rsqrt_fusion.1) | copy-start | bytes 3076
  10.5 733.6 %copy-start.2 = (bf16[256,1024]{1,0:T(8,128)(2,1)S(1)}, bf16[256,1024]{1,0:T(8,128)(2,1)}, u32[]{:S(2)}) copy-start(bf16[256,1024]{1,0:T(8,128)(2,1)} %param.13) | copy-start | bytes 1572868
  754.1 7.0 copy-start.23
  756.7 32.1 %all-to-all-start = ((bf16[256,3,1024]{0,1,2:T(4,128)(2,1)}), bf16[256,3,1024]{0,1,2:T(4,128)(2,1)S(1)}, u32[]{:S(2)}, u32[]{:S(2)}) async-start(bf16[256,3,1024]{0,1,2:T(4,128)(2,1)} %copy.92), calls=%async_computation | async-start | bytes 4194304 | tf_op jit(solution)/shard_map/all_to_all | solution.py:26
  760.3 701.9 %all-gather.7.cloned.1.call-start = ((), (), s32[]{:S(2)}) async-start(), calls=%async_computation.9 | async-start | bytes 2105344 | tf_op jit(solution)/shard_map/all_gather | solution.py:178
  827.9 638.3 %all-to-all-start.1 = ((bf16[8,2,16384]{2,1,0:T(2,128)(2,1)}), bf16[8,2,16384]{2,1,0:T(2,128)(2,1)S(1)}, u32[]{:S(2)}, u32[]{:S(2)}) async-start(bf16[8,2,16384]{2,1,0:T(2,128)(2,1)} %reshape.196), calls=%async_computation.1 | async-start | bytes 1048576 | tf_op jit(solution)/shard_map/all_to_all | solution.py:30
  1467.3 15.4 copy-start.19
  1467.5 15.1 copy-start.21
  1468.2 14.5 copy-start.4
  1479.1 15.1 all-to-all-start.2
  1482.6 244.9 %reduce-scatter.5.cloned.1.call-start = ((), (), s32[]{:S(2)}) async-start(), calls=%async_computation.7 | async-start | bytes 2162688 | tf_op jit(solution)/shard_map/reduce_scatter | solution.py:225
  1486.1 358.1 %reduce-scatter.3.cloned.1.call-start = ((), (), s32[]{:S(2)}) async-start(), calls=%async_computation.6 | async-start | bytes 8650752 | tf_op jit(solution)/shard_map/reduce_scatter | solution.py:222
  1514.4 2.0 copy-start.1
  1532.9 2.0 copy-start.1
  1545.4 2.1 copy-start.1
  1563.9 2.0 copy-start.1
  1576.5 2.1 copy-start.1
  1589.0 2.1 copy-start.1
  1607.6 2.0 copy-start.1
  1620.1 2.1 copy-start.1
  1632.7 2.1 copy-start.1
  1645.2 2.1 copy-start.1
  1648.9 11.9 copy-start.10
  1705.0 2.5 copy-start.9
  1707.5 2.8 copy-start.3
  1707.5 2.8 copy-start.16
  1707.5 2.8 copy-start.18
  1716.1 217.0 %all-reduce.5.cloned.1.call-start = ((), (), s32[]{:S(2)}) async-start(), calls=%async_computation.10 | async-start | bytes 655360
  1718.0 3.5 copy-start.7
  1721.5 122.8 %copy-start.14 = (bf16[256,1024]{1,0:T(8,128)(2,1)S(1)}, bf16[256,1024]{1,0:T(8,128)(2,1)}, u32[]{:S(2)}) copy-start(bf16[256,1024]{1,0:T(8,128)(2,1)} %param.17) | copy-start | bytes 1572868
  (19 other events, 27.5 us)
Sparse Core Ops, SparseCore 0:
  9.9 721.5 all-gather.4
  763.1 699.1 all-gather.6
  1486.2 118.4 reduce-scatter.4
  1716.2 127.9 reduce-scatter.2
  1847.0 86.1 all-reduce.4
where the time goes:
time: 1960 us; the launch traced here: 1940 us
  waiting for transfers between devices  1590 us (81%)
  matrix products  142 us (7%)
  local copies, waits for them, and re-layouts  113 us (6%)
  other arithmetic  30.9 us (2%)
  blocking collectives  30.3 us (2%)
    all_gather x1, waiting for transfers between devices, local(): lax.all_gather(in_weight, ('dp', 'seq'), axis=0, tiled=True)  721 us
    all_gather x1, waiting for transfers between devices, local(): lax.all_gather(out_weight, ('dp', 'seq'), axis=0, tiled=True)  629 us
    reduce_scatter x1, waiting for transfers between devices, local(): lax.psum_scatter(in_partial.astype(jnp.bfloat16), 'dp', scatter_dimension...  117 us
    unnamed x6, waiting for transfers between devices  89 us
  transfers between devices with their start and end apart: 8, of which 6 were waited for; matrix products, arithmetic and copies ran while one was open for 12% of the time, Pallas kernels for 0%

commit v1 on v0

v1 whole, which is shorter than its diff:
```python
import functools

import jax
import jax.numpy as jnp
from jax import lax
from jax.experimental import pallas as pl
from jax.experimental.pallas import tpu as pltpu
from jax.sharding import PartitionSpec as P

F32 = jnp.float32
BF16 = jnp.bfloat16
MESH = pl.DeviceIdType.MESH
DMA = pltpu.SemaphoreType.DMA

D = 1024
HEADS = 8
HD = 128
ROWS = 256
NZ = 8
epsilon = 1e-05
HALF_FACTOR = 0.5 * HD ** (-0.5)
VMEM = pl.BlockSpec(memory_space=pltpu.VMEM)
ABT = (((1,), (1,)), ((), ()))
ATB = (((0,), (0,)), ((), ()))


def dot(a, b, dims=(((1,), (0,)), ((), ()))):
    return lax.dot_general(a, b, dims, preferred_element_type=F32)


class Place:
    def __init__(self):
        g = lax.axis_index("dp")
        s = lax.axis_index("seq")
        self.z, self.ylo, self.k = g // 4, (g // 2) % 2, g % 2
        self.yhi, self.x = s // 4, s % 4
        self.w = self.k * 4 + self.x
        self.head = 2 * self.x + self.k
        self.moved = self.k != self.yhi

    def device(self, z=None, ylo=None, k=None, yhi=None, x=None):
        z = self.z if z is None else z
        ylo = self.ylo if ylo is None else ylo
        k = self.k if k is None else k
        yhi = self.yhi if yhi is None else yhi
        x = self.x if x is None else x
        return (z * 4 + ylo * 2 + k, yhi * 4 + x)

    def row(self, dk, dx):
        return (self.k + dk) % 2, (self.x + dx) % 4

    def along_z(self, d):
        return (self.z + d) % NZ

    def along_y(self, d):
        y = (self.yhi * 2 + self.ylo + d) % 4
        return y // 2, y % 2

    def partner(self):
        return self.device(k=self.yhi, yhi=self.k)

    def sibling(self):
        return self.device(k=1 - self.k)

    def row_peers(self):
        peers = []
        for d in range(1, 8):
            k, x = self.row(d // 4, d % 4)
            peers.append(self.device(k=k, x=x))
        return peers

    def zy_peers(self):
        peers = [self.device(z=self.along_z(d)) for d in range(1, NZ)]
        for d in range(1, 4):
            yhi, ylo = self.along_y(d)
            peers.append(self.device(ylo=ylo, yhi=yhi))
        return peers


def greet(me, peers, with_partner):
    barrier = pltpu.get_barrier_semaphore()
    for peer in peers:
        pl.semaphore_signal(barrier, inc=1, device_id=peer, device_id_type=MESH)
    if with_partner:

        @pl.when(me.moved)
        def _():
            pl.semaphore_signal(barrier, inc=1, device_id=me.partner(), device_id_type=MESH)

    if with_partner:
        pl.semaphore_wait(barrier, len(peers) + me.moved.astype(jnp.int32))
    else:
        pl.semaphore_wait(barrier, len(peers))


def copy(src, dst, send, recv, to):
    return pltpu.make_async_remote_copy(
        src_ref=src, dst_ref=dst, send_sem=send, recv_sem=recv, device_id=to, device_id_type=MESH
    )


class Sends:
    def __init__(self):
        self.started = []

    def push(self, src, dst, send, recv, to):
        one = copy(src, dst, send, recv, to)
        one.start()
        self.started.append(one)

    def drain(self):
        for one in self.started:
            one.wait_send()


def arrived(ref, send, recv, me):
    copy(ref, ref, send, recv, me.sibling()).wait_recv()


def normalize(values):
    centre = values - jnp.mean(values, axis=-1, keepdims=True)
    inverse = lax.rsqrt(jnp.mean(centre * centre, axis=-1, keepdims=True) + epsilon)
    return centre * inverse, inverse


def gather_kernel(
    tok, cot, wi, wo, lens,
    normed, gated, slope, win, wout, dmix, tokr, cotr, lens_out,
    wi_f, wi_send, wi_recv, wi_asm, wo_f, wo_send, wo_recv, wo_asm, dsend, len_send, len_recv,
    swap_s, swap_r, xi_s, xi_r, xo_s, xo_r, zi_s, zi_r, zo_s, zo_r, yi_s, yi_r, yo_s, yo_r, core_s, core_r,
    ag_s, ag_r, fw_s, dm_s, dm_r,
):
    me = Place()
    z, ylo, k, yhi, x, w = me.z, me.ylo, me.k, me.yhi, me.x, me.w
    sends = Sends()
    greet(me, me.row_peers() + me.zy_peers(), True)

    swap_tok = copy(tok, tokr, swap_s.at[0], swap_r.at[0], me.partner())
    swap_cot = copy(cot, cotr, swap_s.at[1], swap_r.at[1], me.partner())

    @pl.when(me.moved)
    def _():
        swap_tok.start()

    @pl.when(jnp.logical_not(me.moved))
    def _():
        tokr[...] = tok[...]
        cotr[...] = cot[...]

    len_send[...] = jnp.zeros_like(len_send)
    len_send[0:1, 0:4] = lens[...]
    sends.push(len_send, len_recv, swap_s.at[2], swap_r.at[2], me.sibling())

    wide = wi[...].astype(F32)
    for h in range(HEADS):
        for b in range(4):
            wi_f[h, b * 4 : b * 4 + 4, :] = wide[:, b * D + h * HD : b * D + (h + 1) * HD]
    wi_send[...] = wi_f[...].astype(BF16)
    for d in range(1, 8):
        pk, px = me.row(d // 4, d % 4)
        sends.push(
            wi_send.at[2 * px + pk], wi_recv.at[w], xi_s.at[d - 1], xi_r.at[d - 1], me.device(k=pk, x=px)
        )
    wi_recv[w] = wi_send[me.head]
    wide_o = wo[...].astype(F32)
    for b in range(8):
        wo_f[b * 4 : b * 4 + 4, :] = wide_o[:, b * HD : (b + 1) * HD]
    wo_send[...] = wo_f[...].astype(BF16)
    for d in range(1, 4):
        pk, px = me.row(0, d)
        sends.push(wo_send, wo_recv.at[x], xo_s.at[d - 1], xo_r.at[d - 1], me.device(x=px))
    wo_recv[x] = wo_send[...]

    def norm_own():
        normed[w] = normalize(tokr[...].astype(F32))[0].astype(BF16)

    def send_own():
        right, left = me.device(x=(x + 1) % 4), me.device(x=(x + 3) % 4)
        for step in range(2):
            for to, half, slot in ((right, step, 3), (left, 1 - step, 1)):
                part = normed.at[w, pl.ds(half * 128, 128)]
                sends.push(part, part, ag_s.at[slot, half], ag_r.at[slot, half], to)
        for half in range(2):
            part = normed.at[w, pl.ds(half * 128, 128)]
            sends.push(part, part, fw_s.at[0, half], ag_r.at[4, half], me.sibling())

    @pl.when(jnp.logical_not(me.moved))
    def _():
        norm_own()

    for d in range(1, 8):
        pk, px = me.row(d // 4, d % 4)
        sk, sx = (k + 2 - d // 4) % 2, (x + 4 - d % 4) % 4
        arrived(wi_recv.at[sk * 4 + sx], xi_s.at[d - 1], xi_r.at[d - 1], me)
    for src in range(8):
        piece = wi_recv[src].astype(F32)
        for b in range(4):
            wi_asm[src // 4, (src % 4) * 4 : (src % 4) * 4 + 4, b * HD : (b + 1) * HD] = piece[b * 4 : b * 4 + 4]
    for c in range(2):
        win[z, ylo, c, yhi] = wi_asm[c].astype(BF16)
    for d in range(1, NZ):
        part = win.at[z, ylo, :, yhi]
        sends.push(part, part, zi_s.at[d - 1], zi_r.at[d - 1], me.device(z=me.along_z(d)))

    @pl.when(me.moved)
    def _():
        swap_tok.wait_recv()
        norm_own()

    send_own()

    @pl.when(me.moved)
    def _():
        swap_cot.start()

    for d in range(1, 4):
        arrived(wo_recv.at[(x + 4 - d) % 4], xo_s.at[d - 1], xo_r.at[d - 1], me)
    for src in range(4):
        piece = wo_recv[src].astype(F32)
        for b in range(8):
            wo_asm[src * 4 : src * 4 + 4, b * HD : (b + 1) * HD] = piece[b * 4 : b * 4 + 4]
    wout[z, ylo, k, yhi] = wo_asm[...].astype(BF16)
    for d in range(1, NZ):
        part = wout.at[z, ylo, k, yhi]
        sends.push(part, part, zo_s.at[d - 1], zo_r.at[d - 1], me.device(z=me.along_z(d)))

    def rows_of(dx, half):
        return normed.at[k * 4 + (x + dx) % 4, pl.ds(half * 128, 128)]

    def take(dx, half):
        part = rows_of(dx, half)
        arrived(part, ag_s.at[dx, half], ag_r.at[dx, half], me)
        sends.push(part, part, fw_s.at[dx, half], ag_r.at[4 + dx, half], me.sibling())

    take(3, 0)
    part = rows_of(3, 0)
    sends.push(part, part, ag_s.at[2, 0], ag_r.at[2, 0], me.device(x=(x + 1) % 4))
    take(1, 1)
    part = rows_of(1, 1)
    sends.push(part, part, ag_s.at[2, 1], ag_r.at[2, 1], me.device(x=(x + 3) % 4))

    for d in range(1, NZ):
        arrived(win.at[(z + NZ - d) % NZ, ylo, :, yhi], zi_s.at[d - 1], zi_r.at[d - 1], me)
    for d in range(1, 4):
        phi, plo = me.along_y(d)
        part = win.at[:, ylo, :, yhi]
        sends.push(part, part, yi_s.at[d - 1], yi_r.at[d - 1], me.device(ylo=plo, yhi=phi))
    take(3, 1)
    take(1, 0)
    for d in range(1, NZ):
        arrived(wout.at[(z + NZ - d) % NZ, ylo, k, yhi], zo_s.at[d - 1], zo_r.at[d - 1], me)
    for d in range(1, 4):
        phi, plo = me.along_y(d)
        part = wout.at[:, ylo, k, yhi]
        sends.push(part, part, yo_s.at[d - 1], yo_r.at[d - 1], me.device(ylo=plo, yhi=phi))
    take(2, 0)
    take(2, 1)
    for d in range(1, 4):
        shi, slo = me.along_y(4 - d)
        arrived(win.at[:, slo, :, shi], yi_s.at[d - 1], yi_r.at[d - 1], me)

    def project(block):
        left = normed[block]
        for n in range(2):
            cols = pl.ds(n * 256, 256)
            hidden = dot(left, win[:, :, :, :, :, cols].reshape(D, 256))
            sigma = 0.5 + 0.5 * jnp.tanh(0.5 * hidden)
            value = hidden * sigma
            gated[block, :, cols] = value.astype(BF16)
            slope[block, :, cols] = (sigma + value * (1.0 - sigma)).astype(BF16)

    @pl.loop(0, 4)
    def _(i):
        project(k * 4 + i)

    for dx in range(4):
        for half in range(2):
            arrived(
                normed.at[(1 - k) * 4 + (x + dx) % 4, pl.ds(half * 128, 128)],
                fw_s.at[dx, half], ag_r.at[4 + dx, half], me,
            )

    @pl.loop(0, 4)
    def _(i):
        project((1 - k) * 4 + i)

    for d in range(1, 4):
        shi, slo = me.along_y(4 - d)
        arrived(wout.at[:, slo, k, shi], yo_s.at[d - 1], yo_r.at[d - 1], me)
    sends.push(wout.at[:, :, k], wout.at[:, :, k], core_s, core_r, me.sibling())

    @pl.when(me.moved)
    def _():
        swap_cot.wait_recv()

    arrived(wout.at[:, :, 1 - k], core_s, core_r, me)

    @pl.loop(0, 4)
    def _(i):
        pair = dot(cotr[...], wout[pl.ds(2 * i, 2)].reshape(256, D), ABT)
        dsend[2 * i] = pair[:, :HD].astype(BF16)
        dsend[2 * i + 1] = pair[:, HD:].astype(BF16)

    dmix[w] = dsend[me.head]
    for d in range(1, 8):
        pk, px = me.row(d // 4, d % 4)
        sends.push(dsend.at[2 * px + pk], dmix.at[w], dm_s.at[d - 1], dm_r.at[d - 1], me.device(k=pk, x=px))
    for d in range(1, 8):
        sk, sx = (k + 2 - d // 4) % 2, (x + 4 - d % 4) % 4
        arrived(dmix.at[sk * 4 + sx], dm_s.at[d - 1], dm_r.at[d - 1], me)
    arrived(len_recv, swap_s.at[2], swap_r.at[2], me)
    lens_out[...] = jnp.where(me.moved, len_recv[...], len_send[...])
    sends.drain()

    @pl.when(me.moved)
    def _():
        swap_tok.wait_send()
        swap_cot.wait_send()


def run_gather(tok, cot, wi, wo, lens):
    shapes = [
        ((8, ROWS, D), BF16), ((8, ROWS, 512), BF16), ((8, ROWS, 512), BF16),
        ((NZ, 2, 2, 2, 16, 512), BF16), ((NZ, 2, 2, 2, 16, D), BF16), ((8, ROWS, HD), BF16),
        ((ROWS, D), BF16), ((ROWS, D), BF16), ((8, 128), jnp.int32),
    ]
    scratch = [
        pltpu.VMEM((8, 16, 128), F32), pltpu.VMEM((8, 16, 128), BF16), pltpu.VMEM((8, 16, 128), BF16),
        pltpu.VMEM((2, 16, 512), F32),
        pltpu.VMEM((32, 128), F32), pltpu.VMEM((32, 128), BF16), pltpu.VMEM((4, 32, 128), BF16),
        pltpu.VMEM((16, D), F32), pltpu.VMEM((8, ROWS, HD), BF16),
        pltpu.VMEM((8, 128), jnp.int32), pltpu.VMEM((8, 128), jnp.int32),
        DMA((3,)), DMA((3,)), DMA((7,)), DMA((7,)), DMA((3,)), DMA((3,)),
        DMA((7,)), DMA((7,)), DMA((7,)), DMA((7,)), DMA((3,)), DMA((3,)), DMA((3,)), DMA((3,)), DMA, DMA,
        DMA((4, 2)), DMA((8, 2)), DMA((4, 2)), DMA((7,)), DMA((7,)),
    ]
    return pl.pallas_call(
        gather_kernel,
        out_shape=[jax.ShapeDtypeStruct(s, t) for s, t in shapes],
        in_specs=[VMEM] * 5,
        out_specs=[VMEM] * len(shapes),
        scratch_shapes=scratch,
        compiler_params=pltpu.CompilerParams(
            collective_id=0, has_side_effects=True, vmem_limit_bytes=48 << 20
        ),
        name="gather",
    )(tok, cot, wi, wo, lens)


def first_of(position, lens):
    e0 = lens[0:1, 0:1]
    e1 = e0 + lens[0:1, 1:2]
    e2 = e1 + lens[0:1, 2:3]
    zero = jnp.zeros_like(position)
    start = jnp.where(position >= e0, e0, zero)
    start = jnp.where(position >= e1, e1, start)
    return jnp.where(position >= e2, e2, start)


def attend_kernel(gated, dmix, lens, attn, stats):
    def block(i, reach):
        query = gated[i, :, 256:384]
        pos = i * ROWS + lax.broadcasted_iota(jnp.int32, (ROWS, 1), 0)
        start = first_of(pos, lens)
        total = jnp.zeros((ROWS, HD), F32)
        for off in range(reach + 1):
            j = i - off
            half = dot(query, gated[j, :, 384:512], ABT) * HALF_FACTOR
            weights = half + half * jnp.tanh(half)
            other = j * ROWS + lax.broadcasted_iota(jnp.int32, (ROWS, ROWS), 1)
            allowed = other >= start
            if off == 0:
                allowed = allowed & (other <= pos)
            weights = jnp.where(allowed, weights, 0.0).astype(BF16)
            total = total + dot(weights, gated[j, :, 128:256])
        rounded = total.astype(BF16)
        attn[i] = rounded
        value = rounded.astype(F32)
        upstream = dmix[i].astype(F32) * gated[i, :, 0:128].astype(F32)
        mean = jnp.mean(value, axis=-1, keepdims=True)
        centre = value - mean
        parts = (
            mean,
            jnp.sum(centre * centre, axis=-1, keepdims=True),
            jnp.sum(upstream, axis=-1, keepdims=True),
            jnp.sum(upstream * centre, axis=-1, keepdims=True),
        )
        lane = lax.broadcasted_iota(jnp.int32, (ROWS, HD), 1)
        packed = jnp.zeros((ROWS, HD), F32)
        for n, part in enumerate(parts):
            packed = jnp.where(lane == n, part, packed)
        stats[i] = packed.T[0:8]

    for i in range(4):
        block(i, i)

    @pl.loop(4, 8)
    def _(i):
        block(i, 4)


def run_attend(gated, dmix, lens):
    return pl.pallas_call(
        attend_kernel,
        out_shape=[jax.ShapeDtypeStruct((8, ROWS, HD), BF16), jax.ShapeDtypeStruct((8, 8, ROWS), F32)],
        in_specs=[VMEM] * 3,
        out_specs=[VMEM] * 2,
        compiler_params=pltpu.CompilerParams(vmem_limit_bytes=32 << 20),
        name="attend",
    )(gated, dmix, lens)


def middle_kernel(
    attn, stats, gated, slope, dmix, dattn, dupper, mixed, every, comb, msend, st_s, st_r, mx_s, mx_r
):
    me = Place()
    k, x, w = me.k, me.x, me.w
    sends = Sends()
    greet(me, me.row_peers(), False)
    for d in range(1, 8):
        pk, px = me.row(d // 4, d % 4)
        sends.push(stats, every.at[w], st_s.at[d - 1], st_r.at[d - 1], me.device(k=pk, x=px))
    every[w] = stats[...]
    for d in range(1, 8):
        sk, sx = (k + 2 - d // 4) % 2, (x + 4 - d % 4) % 4
        arrived(every.at[sk * 4 + sx], st_s.at[d - 1], st_r.at[d - 1], me)

    def block(i):
        mean, second, total, cross = (every[:, i, n, :] for n in range(4))
        middle = jnp.mean(mean, axis=0, keepdims=True)
        apart = mean - middle
        variance = jnp.sum(second + HD * apart * apart, axis=0, keepdims=True) / D
        inverse = lax.rsqrt(variance + epsilon)
        first = jnp.sum(total, axis=0, keepdims=True) / D
        other = inverse * jnp.sum(cross + apart * total, axis=0, keepdims=True) / D
        comb[0:1, :] = middle
        comb[1:2, :] = inverse
        comb[2:3, :] = first
        comb[3:4, :] = other
        turned = comb[...].T
        middle, inverse, first, other = (turned[:, n : n + 1] for n in range(4))
        upper = gated[i, :, 0:128].astype(F32)
        through = dmix[i].astype(F32)
        normal = (attn[i].astype(F32) - middle) * inverse
        msend[i] = (normal * upper).astype(BF16)
        upstream = through * upper
        dattn[i] = (inverse * (upstream - first - normal * other)).astype(BF16)
        dupper[i] = (through * normal * slope[i, :, 0:128].astype(F32)).astype(BF16)

    comb[...] = jnp.zeros_like(comb)

    @pl.loop(0, 8)
    def _(i):
        block(i)

    mixed[me.head] = msend[w]
    for d in range(1, 8):
        pk, px = me.row(d // 4, d % 4)
        sends.push(msend.at[pk * 4 + px], mixed.at[me.head], mx_s.at[d - 1], mx_r.at[d - 1], me.device(k=pk, x=px))
    for d in range(1, 8):
        sk, sx = (k + 2 - d // 4) % 2, (x + 4 - d % 4) % 4
        arrived(mixed.at[2 * sx + sk], mx_s.at[d - 1], mx_r.at[d - 1], me)
    sends.drain()


def run_middle(attn, stats, gated, slope, dmix):
    shape = jax.ShapeDtypeStruct((8, ROWS, HD), BF16)
    return pl.pallas_call(
        middle_kernel,
        out_shape=[shape] * 3,
        in_specs=[VMEM] * 5,
        out_specs=[VMEM] * 3,
        scratch_shapes=[
            pltpu.VMEM((8, 8, 8, ROWS), F32), pltpu.VMEM((128, ROWS), F32), pltpu.VMEM((8, ROWS, HD), BF16),
            DMA((7,)), DMA((7,)), DMA((7,)), DMA((7,)),
        ],
        compiler_params=pltpu.CompilerParams(
            collective_id=1, has_side_effects=True, vmem_limit_bytes=32 << 20
        ),
        name="middle",
    )(attn, stats, gated, slope, dmix)


def back_kernel(gated, slope, dattn, dupper, lens, dhidden, dquery):
    dquery[...] = jnp.zeros_like(dquery)
    dhidden[:, :, 0:128] = dupper[...]

    def block(j, reach):
        key = gated[j, :, 384:512]
        value = gated[j, :, 128:256]
        other = j * ROWS + lax.broadcasted_iota(jnp.int32, (ROWS, ROWS), 0)
        dkey = jnp.zeros((ROWS, HD), F32)
        dvalue = jnp.zeros((ROWS, HD), F32)
        for off in range(reach + 1):
            i = j + off
            query = gated[i, :, 256:384]
            grad = dattn[i]
            half = dot(key, query, ABT) * HALF_FACTOR
            pos = i * ROWS + lax.broadcasted_iota(jnp.int32, (1, ROWS), 1)
            allowed = other >= first_of(pos, lens)
            if off == 0:
                allowed = allowed & (other <= pos)
            double = jnp.where(allowed, 1.0 + jnp.tanh(half), 0.0)
            weights = half * double
            bend = double + weights * (2.0 - double)
            dscores = (dot(value, grad, ABT) * bend).astype(BF16)
            dvalue = dvalue + dot(weights.astype(BF16), grad)
            dkey = dkey + dot(dscores, query)
            dquery[i] += dot(dscores, key, ATB)
        dhidden[j, :, 128:256] = (dvalue * slope[j, :, 128:256].astype(F32)).astype(BF16)
        dhidden[j, :, 384:512] = (dkey * HALF_FACTOR * slope[j, :, 384:512].astype(F32)).astype(BF16)

    @pl.loop(0, 4)
    def _(j):
        block(j, 4)

    for j in range(4, 8):
        block(j, 7 - j)

    @pl.loop(0, 8)
    def _(i):
        dhidden[i, :, 256:384] = (dquery[i] * HALF_FACTOR * slope[i, :, 256:384].astype(F32)).astype(BF16)


def run_back(gated, slope, dattn, dupper, lens):
    return pl.pallas_call(
        back_kernel,
        out_shape=jax.ShapeDtypeStruct((8, ROWS, 512), BF16),
        in_specs=[VMEM] * 5,
        out_specs=VMEM,
        scratch_shapes=[pltpu.VMEM((8, ROWS, HD), F32)],
        compiler_params=pltpu.CompilerParams(vmem_limit_bytes=32 << 20),
        name="back",
    )(gated, slope, dattn, dupper, lens)


def reduce_kernel(
    normed, dhidden, win, wout, mixed, tokr, cotr,
    layer_out, tok_grad, wi_grad, wo_grad,
    lay, grad, esum, es_send, es_recv, x2_send, rl_recv, nb_send, nb_recv,
    gs, gy, gz_send, gz, gx_f, gx_recv, ps, pc, pk_sum, py, pz_send, pz, px_f, px_recv,
    sib_s, sib_r, rl_s, rl_r, nb_s, nb_r, gy_s, gy_r, gz_s, gz_r, gx_s, gx_r,
    pc_s, pc_r, py_s, py_r, pz_s, pz_r, px_s, px_r, sw_s, sw_r,
):
    me = Place()
    z, ylo, k, yhi, x, w = me.z, me.ylo, me.k, me.yhi, me.x, me.w
    sends = Sends()
    greet(me, me.row_peers() + me.zy_peers(), True)
    right, left = me.device(x=(x + 1) % 4), me.device(x=(x + 3) % 4)

    def back_product(block, n):
        return dot(dhidden[block], win[pl.ds(2 * n, 2)].reshape(256, 512), ABT)

    def partial(dx):
        there = (1 - k) * 4 + (x + dx) % 4
        here = k * 4 + (x + dx) % 4

        @pl.loop(0, 4)
        def _(n):
            cols = pl.ds(pl.multiple_of(n * 256, 256), 256)
            es_send[dx, :, cols] = back_product(there, n).astype(BF16)

        sends.push(es_send.at[dx], es_recv.at[dx], sib_s.at[dx], sib_r.at[dx], me.sibling())

        @pl.loop(0, 4)
        def _(n):
            cols = pl.ds(pl.multiple_of(n * 256, 256), 256)
            esum[dx, :, cols] = back_product(here, n)

    def from_sibling(dx):
        arrived(es_recv.at[dx], sib_s.at[dx], sib_r.at[dx], me)

    partial(2)
    partial(1)
    from_sibling(2)
    x2_send[...] = (esum[2] + es_recv[2].astype(F32)).astype(BF16)
    sends.push(x2_send.at[pl.ds(0, 128)], rl_recv.at[0], rl_s.at[0], rl_r.at[0], right)
    sends.push(x2_send.at[pl.ds(128, 128)], rl_recv.at[1], rl_s.at[1], rl_r.at[1], left)
    partial(3)

    from_sibling(1)
    nb_send[0, 128:256] = (esum[1, 128:256] + es_recv[1, 128:256].astype(F32)).astype(BF16)
    sends.push(nb_send.at[0, pl.ds(128, 128)], nb_recv.at[0, pl.ds(128, 128)], nb_s.at[0, 1], nb_r.at[0, 1], right)
    from_sibling(3)
    nb_send[1, 0:128] = (esum[3, 0:128] + es_recv[3, 0:128].astype(F32)).astype(BF16)
    sends.push(nb_send.at[1, pl.ds(0, 128)], nb_recv.at[1, pl.ds(0, 128)], nb_s.at[1, 0], nb_r.at[1, 0], left)

    @pl.loop(0, 4)
    def _(n):
        cols = pl.ds(pl.multiple_of(n * 256, 256), 256)
        product = dot(normed[:, :, cols].reshape(8 * ROWS, 256), dhidden[...].reshape(8 * ROWS, 512), ATB)
        gs[pl.ds(2 * n, 2)] = product.astype(BF16).reshape(2, 2, 2, 2, 16, 512)

    for d in range(1, 4):
        phi, plo = me.along_y(d)
        sends.push(gs.at[:, plo, :, phi], gy.at[d - 1], gy_s.at[d - 1], gy_r.at[d - 1], me.device(ylo=plo, yhi=phi))

    arrived(rl_recv.at[0], rl_s.at[0], rl_r.at[0], me)
    nb_send[0, 0:128] = (
        esum[1, 0:128] + es_recv[1, 0:128].astype(F32) + rl_recv[0].astype(F32)
    ).astype(BF16)
    sends.push(nb_send.at[0, pl.ds(0, 128)], nb_recv.at[0, pl.ds(0, 128)], nb_s.at[0, 0], nb_r.at[0, 0], right)
    arrived(rl_recv.at[1], rl_s.at[1], rl_r.at[1], me)
    nb_send[1, 128:256] = (
        esum[3, 128:256] + es_recv[3, 128:256].astype(F32) + rl_recv[1].astype(F32)
    ).astype(BF16)
    sends.push(nb_send.at[1, pl.ds(128, 128)], nb_recv.at[1, pl.ds(128, 128)], nb_s.at[1, 1], nb_r.at[1, 1], left)
    partial(0)

    @pl.loop(0, 4)
    def _(n):
        pair = jnp.concatenate([mixed[2 * n], mixed[2 * n + 1]], axis=1)
        product = dot(pair, cotr[...], ATB)
        ps[pl.ds(2 * n, 2)] = product.astype(BF16).reshape(2, 2, 2, 2, 16, D)

    sends.push(ps.at[:, :, 1 - k], pc, pc_s, pc_r, me.sibling())

    joined = jnp.concatenate([mixed[h] for h in range(HEADS)], axis=1)
    for n in range(4):
        cols = pl.ds(n * 256, 256)
        product = dot(joined, wout[:, :, :, :, :, cols].reshape(D, 256))
        lay[:, cols] = (product + tokr[:, cols].astype(F32)).astype(BF16)
    swap_lay = copy(lay, layer_out, sw_s.at[0], sw_r.at[0], me.partner())
    swap_grad = copy(grad, tok_grad, sw_s.at[1], sw_r.at[1], me.partner())

    @pl.when(me.moved)
    def _():
        swap_lay.start()

    @pl.when(jnp.logical_not(me.moved))
    def _():
        layer_out[...] = lay[...]

    arrived(pc, pc_s, pc_r, me)

    @pl.loop(0, NZ)
    def _(n):
        pk_sum[n] = (ps[n, :, k].astype(F32) + pc[n].astype(F32)).astype(BF16)

    for d in range(1, 4):
        phi, plo = me.along_y(d)
        sends.push(pk_sum.at[:, plo, phi], py.at[d - 1], py_s.at[d - 1], py_r.at[d - 1], me.device(ylo=plo, yhi=phi))

    for d in range(1, 4):
        arrived(gy.at[d - 1], gy_s.at[d - 1], gy_r.at[d - 1], me)

    @pl.loop(0, NZ)
    def _(n):
        total = gs[n, ylo, :, yhi].astype(F32)
        for d in range(3):
            total = total + gy[d, n].astype(F32)
        gz_send[n] = total.astype(BF16)

    for d in range(1, NZ):
        to = me.along_z(d)
        sends.push(gz_send.at[to], gz.at[d - 1], gz_s.at[d - 1], gz_r.at[d - 1], me.device(z=to))

    from_sibling(0)
    for side, half in ((0, 1), (1, 0), (0, 0), (1, 1)):
        arrived(nb_recv.at[side, pl.ds(half * 128, 128)], nb_s.at[side, half], nb_r.at[side, half], me)

    @pl.loop(0, 4)
    def _(n):
        part = pl.ds(pl.multiple_of(n * 64, 64), 64)
        upstream = (
            esum[0, part]
            + es_recv[0, part].astype(F32)
            + nb_recv[0, part].astype(F32)
            + nb_recv[1, part].astype(F32)
        )
        normal, inverse = normalize(tokr[part].astype(F32))
        first = jnp.mean(upstream, axis=-1, keepdims=True)
        second = jnp.mean(upstream * normal, axis=-1, keepdims=True)
        grad[part] = (inverse * (upstream - first - normal * second) + cotr[part].astype(F32)).astype(BF16)

    @pl.when(me.moved)
    def _():
        swap_grad.start()

    @pl.when(jnp.logical_not(me.moved))
    def _():
        tok_grad[...] = grad[...]

    for d in range(1, 4):
        arrived(py.at[d - 1], py_s.at[d - 1], py_r.at[d - 1], me)

    @pl.loop(0, NZ)
    def _(n):
        total = pk_sum[n, ylo, yhi].astype(F32)
        for d in range(3):
            total = total + py[d, n].astype(F32)
        pz_send[n] = total.astype(BF16)

    for d in range(1, NZ):
        to = me.along_z(d)
        sends.push(pz_send.at[to], pz.at[d - 1], pz_s.at[d - 1], pz_r.at[d - 1], me.device(z=to))

    for d in range(1, NZ):
        arrived(gz.at[d - 1], gz_s.at[d - 1], gz_r.at[d - 1], me)
    total = gz_send[z].astype(F32)
    for d in range(1, NZ):
        total = total + gz[d - 1].astype(F32)
    for c in range(2):
        for px in range(4):
            for b in range(4):
                gx_f[c * 4 + px, b * 4 : b * 4 + 4, :] = total[c, px * 4 : px * 4 + 4, b * HD : (b + 1) * HD]
    gx_recv[w] = gx_f[w]
    for d in range(1, 8):
        pk, px = me.row(d // 4, d % 4)
        sends.push(gx_f.at[pk * 4 + px], gx_recv.at[w], gx_s.at[d - 1], gx_r.at[d - 1], me.device(k=pk, x=px))

    for d in range(1, NZ):
        arrived(pz.at[d - 1], pz_s.at[d - 1], pz_r.at[d - 1], me)
    total = pz_send[z].astype(F32)
    for d in range(1, NZ):
        total = total + pz[d - 1].astype(F32)
    for px in range(4):
        for b in range(8):
            px_f[px, b * 4 : b * 4 + 4, :] = total[px * 4 : px * 4 + 4, b * HD : (b + 1) * HD]
    px_recv[x] = px_f[x]
    for d in range(1, 4):
        pk, px = me.row(0, d)
        sends.push(px_f.at[px], px_recv.at[x], px_s.at[d - 1], px_r.at[d - 1], me.device(x=px))

    for d in range(1, 8):
        sk, sx = (k + 2 - d // 4) % 2, (x + 4 - d % 4) % 4
        arrived(gx_recv.at[sk * 4 + sx], gx_s.at[d - 1], gx_r.at[d - 1], me)
    for src in range(8):
        h = 2 * (src % 4) + src // 4
        for b in range(4):
            wi_grad[:, b * D + h * HD : b * D + (h + 1) * HD] = gx_recv[src, b * 4 : b * 4 + 4, :]
    for d in range(1, 4):
        arrived(px_recv.at[(x + 4 - d) % 4], px_s.at[d - 1], px_r.at[d - 1], me)
    total = px_recv[0] + px_recv[1] + px_recv[2] + px_recv[3]
    for b in range(8):
        wo_grad[:, b * HD : (b + 1) * HD] = total[b * 4 : b * 4 + 4]
    sends.drain()

    @pl.when(me.moved)
    def _():
        swap_lay.wait()
        swap_grad.wait()


def run_reduce(normed, dhidden, win, wout, mixed, tokr, cotr):
    shapes = [((ROWS, D), BF16), ((ROWS, D), BF16), ((4, 4 * D), F32), ((4, D), F32)]
    scratch = [
        pltpu.VMEM((ROWS, D), BF16), pltpu.VMEM((ROWS, D), BF16),
        pltpu.VMEM((4, ROWS, D), F32), pltpu.VMEM((4, ROWS, D), BF16), pltpu.VMEM((4, ROWS, D), BF16),
        pltpu.VMEM((ROWS, D), BF16), pltpu.VMEM((2, 128, D), BF16),
        pltpu.VMEM((2, ROWS, D), BF16), pltpu.VMEM((2, ROWS, D), BF16),
        pltpu.VMEM((NZ, 2, 2, 2, 16, 512), BF16), pltpu.VMEM((3, NZ, 2, 16, 512), BF16),
        pltpu.VMEM((NZ, 2, 16, 512), BF16), pltpu.VMEM((7, 2, 16, 512), BF16),
        pltpu.VMEM((8, 16, 128), F32), pltpu.VMEM((8, 16, 128), F32),
        pltpu.VMEM((NZ, 2, 2, 2, 16, D), BF16), pltpu.VMEM((NZ, 2, 2, 16, D), BF16),
        pltpu.VMEM((NZ, 2, 2, 16, D), BF16), pltpu.VMEM((3, NZ, 16, D), BF16),
        pltpu.VMEM((NZ, 16, D), BF16), pltpu.VMEM((7, 16, D), BF16),
        pltpu.VMEM((4, 32, 128), F32), pltpu.VMEM((4, 32, 128), F32),
        DMA((4,)), DMA((4,)), DMA((2,)), DMA((2,)), DMA((2, 2)), DMA((2, 2)),
        DMA((3,)), DMA((3,)), DMA((7,)), DMA((7,)), DMA((7,)), DMA((7,)),
        DMA, DMA, DMA((3,)), DMA((3,)), DMA((7,)), DMA((7,)), DMA((3,)), DMA((3,)), DMA((2,)), DMA((2,)),
    ]
    return pl.pallas_call(
        reduce_kernel,
        out_shape=[jax.ShapeDtypeStruct(s, t) for s, t in shapes],
        in_specs=[VMEM] * 7,
        out_specs=[VMEM] * 4,
        scratch_shapes=scratch,
        compiler_params=pltpu.CompilerParams(
            collective_id=2, has_side_effects=True, vmem_limit_bytes=56 << 20
        ),
        name="reduce",
    )(normed, dhidden, win, wout, mixed, tokr, cotr)


def local(tokens, lengths, in_weight, out_weight, cotangent):
    normed, gated, slope, win, wout, dmix, tokr, cotr, lens = run_gather(
        tokens, cotangent, in_weight, out_weight, lengths
    )
    attn, stats = run_attend(gated, dmix, lens)
    dattn, dupper, mixed = run_middle(attn, stats, gated, slope, dmix)
    dhidden = run_back(gated, slope, dattn, dupper, lens)
    return tuple(run_reduce(normed, dhidden, win, wout, mixed, tokr, cotr))


def solution(mesh):
    both = P(("dp", "seq"), None)
    return jax.shard_map(
        local,
        mesh=mesh,
        in_specs=(both, P("dp", None), both, both, both),
        out_specs=(both, both, both, both),
        check_vma=False,
    )
```

time: 1960 us -> 183 us (0.09)
  waiting for transfers between devices: 1590 us -> 0 us
  Pallas kernels: 0 us -> 171 us
  matrix products: 142 us -> 0 us
  local copies, waits for them, and re-layouts: 113 us -> 11.3 us
  other arithmetic: 30.9 us -> 0 us
  blocking collectives: 30.3 us -> 0 us
    all_gather x2 -> x0, waiting for transfers between devices: 1350 us -> none  [the longest x1 721 us: local(): lax.all_gather(in_weight, ('dp', 'seq'), axis=0, tiled=True)]
    pallas_call x0 -> x5, Pallas kernels: none -> 171 us  [the longest x1 68.6 us: run_reduce(): pl.pallas_call(reduce_kernel, out_shape=[jax.ShapeDtypeStruct(s, t) for s...]
    dot_general x66 -> x0, matrix products: 142 us -> none  [the longest x10 26.6 us: compute(): jnp.einsum('hqk,qhd->khd', weights, d_query, preferred_element_type=jnp.f...]
    reduce_scatter x2 -> x0, waiting for transfers between devices: 117 us -> none  [the longest x1 117 us: local(): lax.psum_scatter(in_partial.astype(jnp.bfloat16), 'dp', scatter_dimension...]
    unnamed x6 -> x0, waiting for transfers between devices: 89 us -> none
    all_to_all x3 -> x0, waiting for transfers between devices: 35.3 us -> none  [the longest x2 35.3 us: to_heads(): lax.all_to_all(stacked, 'seq', split_axis=2, concat_axis=0, tiled=True)]
    dynamic_slice x68 -> x0, local copies, waits for them, and re-layouts: 31.2 us -> none  [the longest x8 10.2 us: one_query(): query_rows = lax.dynamic_slice_in_dim(queries, q_start, block_rows, 0)]
    all_to_all x1 -> x0, blocking collectives: 30.3 us -> none  [to_tokens(): lax.all_to_all(stacked, 'seq', split_axis=0, concat_axis=2, tiled=True)]
  transfers between devices with their start and end apart: 8 -> 0, of which waited for: 6 -> 0; matrix products, arithmetic and copies ran while one was open for 12% -> 0% of each run, Pallas kernels for 0% -> 0%
where the time goes in v1:
time: 183 us
  Pallas kernels  171 us (93%)
  local copies, waits for them, and re-layouts  11.3 us (6%)
    pallas_call x1, Pallas kernels, run_reduce(): pl.pallas_call(reduce_kernel, out_shape=[jax.ShapeDtypeStruct(s, t) for s...  68.6 us
    pallas_call x1, Pallas kernels, run_gather(): pl.pallas_call(gather_kernel, out_shape=[jax.ShapeDtypeStruct(s, t) for s...  65.5 us
    pallas_call x1, Pallas kernels, run_middle(): pl.pallas_call(middle_kernel, out_shape=[shape] * 3, in_specs=[VMEM] * 5,...  20.3 us
    unnamed x30, local copies, waits for them, and re-layouts  11.3 us
    pallas_call x1, Pallas kernels, run_back(): pl.pallas_call(back_kernel, out_shape=jax.ShapeDtypeStruct((8, ROWS, 512)...  10.9 us
    pallas_call x1, Pallas kernels, run_attend(): pl.pallas_call(attend_kernel, out_shape=[jax.ShapeDtypeStruct((8, ROWS, H...  5.62 us

profile of v1, /device:TPU:1, one launch (start us, length us, event | category | flops | bytes accessed | tf_op | source)
XLA Modules:
  0.0 182.9 jit_solution(544632520271126917)
XLA Ops:
  0.6 0.0 copy-start.3
  0.6 1.0 copy-done.3
  1.7 0.0 copy-start.4
  1.7 1.0 copy-done.4
  2.7 0.8 copy-done.8
  3.5 0.7 copy-done.9
  4.2 0.7 copy-done.10
  4.8 65.5 %gather.1 = (bf16[8,256,1024]{2,1,0:T(8,128)(2,1)}, bf16[8,256,512]{2,1,0:T(8,128)(2,1)S(1)}, bf16[8,256,512]{2,1,0:T(8,128)(2,1)}, bf16[8,2,2,2,16,512]{5,4,3,2...) custom-call(bf16[256,1024]{1,0:T(8,128)(2,1)S(1)} %copy-done.3, ...), custom_call_target="tpu_custom_call" | custom-call | tf_op jit(solution)/shard_map/gather/pallas_call | solution.py:337
  70.3 0.0 copy-start.2
  70.3 0.0 copy-start.5
  70.3 0.0 copy-start.6
  70.3 0.0 copy-start
  70.3 5.6 %attend.1 = (bf16[8,256,128]{2,1,0:T(8,128)(2,1)S(1)}, f32[8,8,256]{2,1,0:T(8,128)S(1)}) custom-call(bf16[8,256,512]{2,1,0:T(8,128)(2,1)S(1)} %get-tuple-element.19.gated, bf16[8,256,128]{2,1,0:T(8,128)(2,1)S(1)} %get-tuple-element.21.dmix, s32[8,128]{1,0:T(8,128)S(1)} %get-tuple-element.22.lens), custom_call_target="tpu_custom_call" | custom-call | tf_op jit(solution)/shard_map/attend/pallas_call | solution.py:403
  76.0 0.0 copy-done
  76.0 20.3 %middle.1 = (bf16[8,256,128]{2,1,0:T(8,128)(2,1)S(1)}, bf16[8,256,128]{2,1,0:T(8,128)(2,1)S(1)}, bf16[8,256,128]{2,1,0:T(8,128)(2,1)S(1)}) custom-call(bf16[8,256,128]{2,1,0:T(8,128)(2,1)S(1)} %get-tuple-element.23.attn, f32[8,8,256]{2,1,0:T(8,128)S(1)} %get-tuple-element.24.stats, bf16[8,256,512]{2,1,0:T(8,128)(2,1)S(1)} %get-tuple-element.19.gated, ...), custom_call_target="tpu_custom_call" | custom-call | tf_op jit(solution)/shard_map/middle/pallas_call | solution.py:468
  96.3 0.0 copy-done.2
  96.3 0.0 copy-done.5
  96.3 0.0 copy-done.6
  96.3 0.0 copy-start.7
  96.3 0.8 copy-done.7
  97.1 10.9 %back.1.dhidden = bf16[8,256,512]{2,1,0:T(8,128)(2,1)S(1)} custom-call(bf16[8,256,512]{2,1,0:T(8,128)(2,1)S(1)} %get-tuple-element.19.gated, bf16[8,256,512]{2,1,0:T(8,128)(2,1)S(1)} %copy-done, bf16[8,256,128]{2,1,0:T(8,128)(2,1)S(1)} %get-tuple-element.25.dattn, bf16[8,256,128]{2,1,0:T(8,128)(2,1)S(1)} %get-tuple-element.26.dupper, ...), custom_call_target="tpu_custom_call" | custom-call | tf_op jit(solution)/shard_map/back/pallas_call | solution.py:526
  107.9 0.0 copy-start.1
  108.0 1.3 copy-done.1
  109.3 68.6 %reduce.1 = (bf16[256,1024]{1,0:T(8,128)(2,1)}, bf16[256,1024]{1,0:T(8,128)(2,1)}, f32[4,4096]{1,0:T(4,128)}, f32[4,1024]{1,0:T(4,128)}) custom-call(bf16[8,256,1024]{2,1,0:T(8,128)(2,1)} %get-tuple-element.18.normed, bf16[8,256,512]{2,1,0:T(8,128)(2,1)} %copy-done.1, bf16[8,2,2,2,16,512]{5,4,3,2,1,0:T(8,128)(2,1)} %copy-done.2, ...), custom_call_target="tpu_custom_call" | custom-call | tf_op jit(solution)/shard_map/reduce/pallas_call | solution.py:763
  177.9 0.0 copy-start.11
  177.9 0.0 copy-start.12
  177.9 1.9 %copy.13 = bf16[256,1024]{1,0:T(8,128)(2,1)} copy(bf16[256,1024]{1,0:T(8,128)(2,1)} %get-tuple-element.36) | data formatting | bytes 1048576
  179.8 1.9 %copy.14 = bf16[256,1024]{1,0:T(8,128)(2,1)} copy(bf16[256,1024]{1,0:T(8,128)(2,1)} %get-tuple-element.37) | data formatting | bytes 1048576
  181.7 0.0 copy-done.11
  181.7 0.6 copy.15
  182.3 0.0 copy-done.12
  182.3 0.6 copy.16
  (3 shorter events, 0.0 us)
Async XLA Ops:
  0.6 1.0 copy-start.3
  1.7 1.0 copy-start.4
  2.7 0.8 copy-start.8
  3.5 0.7 copy-start.9
  4.2 0.7 copy-start.10
  70.3 26.0 %copy-start.2 = (bf16[8,2,2,2,16,512]{5,4,3,2,1,0:T(8,128)(2,1)}, bf16[8,2,2,2,16,512]{5,4,3,2,1,0:T(8,128)(2,1)S(1)}, u32[]{:S(2)}) copy-start(bf16[8,2,2,2,16,512]{5,4,3,2,1,0:T(8,128)(2,1)S(1)} %get-tuple-element.27.win) | copy-start | bytes 3145732
  70.3 26.0 %copy-start.5 = (bf16[256,1024]{1,0:T(8,128)(2,1)}, bf16[256,1024]{1,0:T(8,128)(2,1)S(1)}, u32[]{:S(2)}) copy-start(bf16[256,1024]{1,0:T(8,128)(2,1)S(1)} %get-tuple-element.30.tokr) | copy-start | bytes 1572868
  70.3 26.0 %copy-start.6 = (bf16[256,1024]{1,0:T(8,128)(2,1)}, bf16[256,1024]{1,0:T(8,128)(2,1)S(1)}, u32[]{:S(2)}) copy-start(bf16[256,1024]{1,0:T(8,128)(2,1)S(1)} %get-tuple-element.31.cotr) | copy-start | bytes 1572868
  70.3 5.6 %copy-start = (bf16[8,256,512]{2,1,0:T(8,128)(2,1)S(1)}, bf16[8,256,512]{2,1,0:T(8,128)(2,1)}, u32[]{:S(2)}) copy-start(bf16[8,256,512]{2,1,0:T(8,128)(2,1)} %get-tuple-element.20.slope) | copy-start | bytes 6291460
  96.3 0.8 copy-start.7
  107.9 1.4 copy-start.1
  177.9 3.8 %copy-start.11 = (f32[4,4096]{1,0:T(4,128)S(1)}, f32[4,4096]{1,0:T(4,128)}, u32[]{:S(2)}) copy-start(f32[4,4096]{1,0:T(4,128)} %get-tuple-element.38) | copy-start | bytes 196612
  177.9 4.4 %copy-start.12 = (f32[4,1024]{1,0:T(4,128)S(1)}, f32[4,1024]{1,0:T(4,128)}, u32[]{:S(2)}) copy-start(f32[4,1024]{1,0:T(4,128)} %get-tuple-element.39) | copy-start | bytes 49156

commit v2 on v0

v2 whole, which is shorter than its diff:
```python
import functools

import jax
import jax.numpy as jnp
from jax import lax
from jax.experimental import pallas as pl
from jax.experimental.pallas import tpu as pltpu
from jax.sharding import PartitionSpec as P

F32 = jnp.float32
BF16 = jnp.bfloat16
MESH = pl.DeviceIdType.MESH
DMA = pltpu.SemaphoreType.DMA

D = 1024
HEADS = 8
HD = 128
ROWS = 256
NZ = 8
epsilon = 1e-05
HALF_FACTOR = 0.5 * HD ** (-0.5)
VMEM = pl.BlockSpec(memory_space=pltpu.VMEM)
ABT = (((1,), (1,)), ((), ()))
ATB = (((0,), (0,)), ((), ()))


def dot(a, b, dims=(((1,), (0,)), ((), ()))):
    return lax.dot_general(a, b, dims, preferred_element_type=F32)


class Place:
    def __init__(self):
        g = lax.axis_index("dp")
        s = lax.axis_index("seq")
        self.z, self.ylo, self.k = g // 4, (g // 2) % 2, g % 2
        self.yhi, self.x = s // 4, s % 4
        self.w = self.k * 4 + self.x
        self.head = 2 * self.x + self.k
        self.moved = self.k != self.yhi

    def device(self, z=None, ylo=None, k=None, yhi=None, x=None):
        z = self.z if z is None else z
        ylo = self.ylo if ylo is None else ylo
        k = self.k if k is None else k
        yhi = self.yhi if yhi is None else yhi
        x = self.x if x is None else x
        return (z * 4 + ylo * 2 + k, yhi * 4 + x)

    def row(self, dk, dx):
        return (self.k + dk) % 2, (self.x + dx) % 4

    def along_z(self, d):
        return (self.z + d) % NZ

    def along_y(self, d):
        y = (self.yhi * 2 + self.ylo + d) % 4
        return y // 2, y % 2

    def partner(self):
        return self.device(k=self.yhi, yhi=self.k)

    def sibling(self):
        return self.device(k=1 - self.k)

    def row_peers(self):
        peers = []
        for d in range(1, 8):
            k, x = self.row(d // 4, d % 4)
            peers.append(self.device(k=k, x=x))
        return peers

    def zy_peers(self):
        peers = [self.device(z=self.along_z(d)) for d in range(1, NZ)]
        for d in range(1, 4):
            yhi, ylo = self.along_y(d)
            peers.append(self.device(ylo=ylo, yhi=yhi))
        return peers


def greet(me, peers, with_partner):
    barrier = pltpu.get_barrier_semaphore()
    for peer in peers:
        pl.semaphore_signal(barrier, inc=1, device_id=peer, device_id_type=MESH)
    if with_partner:

        @pl.when(me.moved)
        def _():
            pl.semaphore_signal(barrier, inc=1, device_id=me.partner(), device_id_type=MESH)

    if with_partner:
        pl.semaphore_wait(barrier, len(peers) + me.moved.astype(jnp.int32))
    else:
        pl.semaphore_wait(barrier, len(peers))


def copy(src, dst, send, recv, to):
    return pltpu.make_async_remote_copy(
        src_ref=src, dst_ref=dst, send_sem=send, recv_sem=recv, device_id=to, device_id_type=MESH
    )


class Sends:
    def __init__(self):
        self.started = []

    def push(self, src, dst, send, recv, to):
        one = copy(src, dst, send, recv, to)
        one.start()
        self.started.append(one)

    def drain(self):
        for one in self.started:
            one.wait_send()


def arrived(ref, send, recv, me):
    copy(ref, ref, send, recv, me.sibling()).wait_recv()


def normalize(values):
    centre = values - jnp.mean(values, axis=-1, keepdims=True)
    inverse = lax.rsqrt(jnp.mean(centre * centre, axis=-1, keepdims=True) + epsilon)
    return centre * inverse, inverse


def first_of(position, lens):
    e0 = lens[0:1, 0:1]
    e1 = e0 + lens[0:1, 1:2]
    e2 = e1 + lens[0:1, 2:3]
    zero = jnp.zeros_like(position)
    start = jnp.where(position >= e0, e0, zero)
    start = jnp.where(position >= e1, e1, start)
    return jnp.where(position >= e2, e2, start)


BUFFERS = {
    "tokr": ((ROWS, D), BF16), "cotr": ((ROWS, D), BF16),
    "len_send": ((8, 128), jnp.int32), "len_recv": ((8, 128), jnp.int32), "lens": ((8, 128), jnp.int32),
    "wi_f": ((8, 16, 128), F32), "wi_send": ((8, 16, 128), BF16), "wi_recv": ((8, 16, 128), BF16),
    "wi_asm": ((2, 16, 512), F32),
    "wo_f": ((32, 128), F32), "wo_send": ((32, 128), BF16), "wo_recv": ((4, 32, 128), BF16), "wo_asm": ((16, D), F32),
    "win": ((NZ, 2, 2, 2, 16, 512), BF16), "wout": ((NZ, 2, 2, 2, 16, D), BF16),
    "normed": ((8, ROWS, D), BF16), "gated": ((8, ROWS, 512), BF16), "slope": ((8, ROWS, 512), BF16),
    "dsend": ((8, ROWS, HD), BF16), "dmix": ((8, ROWS, HD), BF16),
    "attn": ((8, ROWS, HD), BF16), "stats": ((8, 8, ROWS), F32), "every": ((8, 8, 8, ROWS), F32),
    "comb": ((128, ROWS), F32), "msend": ((8, ROWS, HD), BF16), "mixed": ((8, ROWS, HD), BF16),
    "dattn": ((8, ROWS, HD), BF16), "dhidden": ((8, ROWS, 512), BF16), "dquery": ((8, ROWS, HD), F32),
    "lay": ((ROWS, D), BF16), "grad": ((ROWS, D), BF16),
    "esum": ((4, ROWS, D), F32), "es_send": ((4, ROWS, D), BF16), "es_recv": ((4, ROWS, D), BF16),
    "x2_send": ((ROWS, D), BF16), "rl_recv": ((2, 128, D), BF16),
    "nb_send": ((2, ROWS, D), BF16), "nb_recv": ((2, ROWS, D), BF16),
    "gs": ((NZ, 2, 2, 2, 16, 512), BF16), "gy": ((3, NZ, 2, 16, 512), BF16),
    "gz_send": ((NZ, 2, 16, 512), BF16), "gz": ((7, 2, 16, 512), BF16),
    "gx_f": ((8, 16, 128), F32), "gx_recv": ((8, 16, 128), F32),
    "ps": ((NZ, 2, 2, 2, 16, D), BF16), "pc": ((NZ, 2, 2, 16, D), BF16), "pk_sum": ((NZ, 2, 2, 16, D), BF16),
    "py": ((3, NZ, 16, D), BF16), "pz_send": ((NZ, 16, D), BF16), "pz": ((7, 16, D), BF16),
    "px_f": ((4, 32, 128), F32), "px_recv": ((4, 32, 128), F32),
}
SEMAPHORES = {
    "load": (2,), "swap": (4,), "xi": (7,), "xo": (3,), "zi": (7,), "zo": (7,), "yi": (3,), "yo": (3,), "core": (1,),
    "ag": (8, 2), "fw": (4, 2), "dm": (7,), "st": (7,), "mx": (7,), "sib": (4,), "rl": (2,), "nb": (2, 2),
    "gy": (3,), "gz": (7,), "gx": (7,), "pc": (1,), "py": (3,), "pz": (7,), "px": (3,), "sw": (2,),
}


class Refs:
    def __init__(self, buffers, semaphores):
        for name, ref in zip(BUFFERS, buffers):
            setattr(self, name, ref)
        for n, name in enumerate(SEMAPHORES):
            setattr(self, name + "_s", semaphores[2 * n])
            setattr(self, name + "_r", semaphores[2 * n + 1])


def project(r, block):
    left = r.normed[block]
    for n in range(2):
        cols = pl.ds(n * 256, 256)
        hidden = dot(left, r.win[:, :, :, :, :, cols].reshape(D, 256))
        sigma = 0.5 + 0.5 * jnp.tanh(0.5 * hidden)
        value = hidden * sigma
        r.gated[block, :, cols] = value.astype(BF16)
        r.slope[block, :, cols] = (sigma + value * (1.0 - sigma)).astype(BF16)


def attend(r, i, reach):
    query = r.gated[i, :, 256:384]
    pos = i * ROWS + lax.broadcasted_iota(jnp.int32, (ROWS, 1), 0)
    start = first_of(pos, r.lens)
    total = jnp.zeros((ROWS, HD), F32)
    for off in range(reach + 1):
        j = i - off
        half = dot(query, r.gated[j, :, 384:512], ABT) * HALF_FACTOR
        weights = half + half * jnp.tanh(half)
        other = j * ROWS + lax.broadcasted_iota(jnp.int32, (ROWS, ROWS), 1)
        allowed = other >= start
        if off == 0:
            allowed = allowed & (other <= pos)
        weights = jnp.where(allowed, weights, 0.0).astype(BF16)
        total = total + dot(weights, r.gated[j, :, 128:256])
    r.attn[i] = total.astype(BF16)


def row_stats(r, i):
    value = r.attn[i].astype(F32)
    upstream = r.dmix[i].astype(F32) * r.gated[i, :, 0:128].astype(F32)
    mean = jnp.mean(value, axis=-1, keepdims=True)
    centre = value - mean
    parts = (
        mean,
        jnp.sum(centre * centre, axis=-1, keepdims=True),
        jnp.sum(upstream, axis=-1, keepdims=True),
        jnp.sum(upstream * centre, axis=-1, keepdims=True),
    )
    lane = lax.broadcasted_iota(jnp.int32, (ROWS, HD), 1)
    packed = jnp.zeros((ROWS, HD), F32)
    for n, part in enumerate(parts):
        packed = jnp.where(lane == n, part, packed)
    r.stats[i] = packed.T[0:8]


def gate_rows(r, i):
    mean, second, total, cross = (r.every[:, i, n, :] for n in range(4))
    middle = jnp.mean(mean, axis=0, keepdims=True)
    apart = mean - middle
    variance = jnp.sum(second + HD * apart * apart, axis=0, keepdims=True) / D
    inverse = lax.rsqrt(variance + epsilon)
    first = jnp.sum(total, axis=0, keepdims=True) / D
    other = inverse * jnp.sum(cross + apart * total, axis=0, keepdims=True) / D
    r.comb[0:1, :] = middle
    r.comb[1:2, :] = inverse
    r.comb[2:3, :] = first
    r.comb[3:4, :] = other
    turned = r.comb[...].T
    middle, inverse, first, other = (turned[:, n : n + 1] for n in range(4))
    upper = r.gated[i, :, 0:128].astype(F32)
    through = r.dmix[i].astype(F32)
    normal = (r.attn[i].astype(F32) - middle) * inverse
    r.msend[i] = (normal * upper).astype(BF16)
    upstream = through * upper
    r.dattn[i] = (inverse * (upstream - first - normal * other)).astype(BF16)
    r.dhidden[i, :, 0:128] = (through * normal * r.slope[i, :, 0:128].astype(F32)).astype(BF16)


def attend_back(r, j, reach):
    key = r.gated[j, :, 384:512]
    value = r.gated[j, :, 128:256]
    other = j * ROWS + lax.broadcasted_iota(jnp.int32, (ROWS, ROWS), 0)
    dkey = jnp.zeros((ROWS, HD), F32)
    dvalue = jnp.zeros((ROWS, HD), F32)
    for off in range(reach + 1):
        i = j + off
        query = r.gated[i, :, 256:384]
        grad = r.dattn[i]
        half = dot(key, query, ABT) * HALF_FACTOR
        pos = i * ROWS + lax.broadcasted_iota(jnp.int32, (1, ROWS), 1)
        allowed = other >= first_of(pos, r.lens)
        if off == 0:
            allowed = allowed & (other <= pos)
        double = jnp.where(allowed, 1.0 + jnp.tanh(half), 0.0)
        weights = half * double
        bend = double + weights * (2.0 - double)
        dscores = (dot(value, grad, ABT) * bend).astype(BF16)
        dvalue = dvalue + dot(weights.astype(BF16), grad)
        dkey = dkey + dot(dscores, query)
        r.dquery[i] += dot(dscores, key, ATB)
    r.dhidden[j, :, 128:256] = (dvalue * r.slope[j, :, 128:256].astype(F32)).astype(BF16)
    r.dhidden[j, :, 384:512] = (dkey * HALF_FACTOR * r.slope[j, :, 384:512].astype(F32)).astype(BF16)


def kernel(tok, cot, wi, wo, lengths, layer_out, tok_grad, wi_grad, wo_grad, *scratch):
    me = Place()
    z, ylo, k, yhi, x, w = me.z, me.ylo, me.k, me.yhi, me.x, me.w
    r = Refs(scratch[: len(BUFFERS)], scratch[len(BUFFERS) :])
    sends = Sends()
    right, left = me.device(x=(x + 1) % 4), me.device(x=(x + 3) % 4)
    stays = jnp.logical_not(me.moved)

    def row_source(d):
        return (k + 2 - d // 4) % 2, (x + 4 - d % 4) % 4

    load_tok = pltpu.make_async_copy(tok, r.tokr, r.load_r.at[0])
    load_cot = pltpu.make_async_copy(cot, r.cotr, r.load_r.at[1])

    @pl.when(stays)
    def _():
        load_tok.start()
        load_cot.start()

    greet(me, me.row_peers() + me.zy_peers(), True)

    swap_tok = [
        copy(tok.at[part], r.tokr.at[part], r.swap_s.at[n], r.swap_r.at[n], me.partner())
        for n, part in ((0, pl.ds(0, 128)), (1, pl.ds(128, 128)))
    ]
    swap_cot = copy(cot, r.cotr, r.swap_s.at[2], r.swap_r.at[2], me.partner())

    @pl.when(me.moved)
    def _():
        swap_tok[0].start()
        swap_tok[1].start()

    wide = wi[...].astype(F32)
    for h in range(HEADS):
        for b in range(4):
            r.wi_f[h, b * 4 : b * 4 + 4, :] = wide[:, b * D + h * HD : b * D + (h + 1) * HD]
    r.wi_send[...] = r.wi_f[...].astype(BF16)
    for d in range(1, 8):
        pk, px = me.row(d // 4, d % 4)
        sends.push(
            r.wi_send.at[2 * px + pk], r.wi_recv.at[w], r.xi_s.at[d - 1], r.xi_r.at[d - 1], me.device(k=pk, x=px)
        )
    r.wi_recv[w] = r.wi_send[me.head]
    wide_o = wo[...].astype(F32)
    for b in range(8):
        r.wo_f[b * 4 : b * 4 + 4, :] = wide_o[:, b * HD : (b + 1) * HD]
    r.wo_send[...] = r.wo_f[...].astype(BF16)
    for d in range(1, 4):
        pk, px = me.row(0, d)
        sends.push(r.wo_send, r.wo_recv.at[x], r.xo_s.at[d - 1], r.xo_r.at[d - 1], me.device(x=px))
    r.wo_recv[x] = r.wo_send[...]
    r.len_send[...] = jnp.zeros_like(r.len_send)
    r.len_send[0:1, 0:4] = lengths[...]
    sends.push(r.len_send, r.len_recv, r.swap_s.at[3], r.swap_r.at[3], me.sibling())

    def norm_half(half):
        part = pl.ds(half * 128, 128)
        r.normed[w, part] = normalize(r.tokr[part].astype(F32))[0].astype(BF16)

    def own(half):
        return r.normed.at[w, pl.ds(half * 128, 128)]

    own_sends = []
    for half in range(2):
        own_sends.append(copy(own(half), own(half), r.ag_s.at[3, half], r.ag_r.at[3, half], right))
        own_sends.append(copy(own(half), own(half), r.ag_s.at[1, half], r.ag_r.at[1, half], left))
        own_sends.append(copy(own(half), own(half), r.fw_s.at[0, half], r.ag_r.at[4, half], me.sibling()))

    @pl.when(stays)
    def _():
        load_tok.wait()
        norm_half(0)
        norm_half(1)
        for n in (0, 4, 3, 1, 2, 5):
            own_sends[n].start()

    for d in range(1, 8):
        sk, sx = row_source(d)
        arrived(r.wi_recv.at[sk * 4 + sx], r.xi_s.at[d - 1], r.xi_r.at[d - 1], me)
    for src in range(8):
        piece = r.wi_recv[src].astype(F32)
        for b in range(4):
            r.wi_asm[src // 4, (src % 4) * 4 : (src % 4) * 4 + 4, b * HD : (b + 1) * HD] = piece[b * 4 : b * 4 + 4]
    for c in range(2):
        r.win[z, ylo, c, yhi] = r.wi_asm[c].astype(BF16)
    for d in range(1, NZ):
        part = r.win.at[z, ylo, :, yhi]
        sends.push(part, part, r.zi_s.at[d - 1], r.zi_r.at[d - 1], me.device(z=me.along_z(d)))

    for d in range(1, 4):
        arrived(r.wo_recv.at[(x + 4 - d) % 4], r.xo_s.at[d - 1], r.xo_r.at[d - 1], me)
    for src in range(4):
        piece = r.wo_recv[src].astype(F32)
        for b in range(8):
            r.wo_asm[src * 4 : src * 4 + 4, b * HD : (b + 1) * HD] = piece[b * 4 : b * 4 + 4]
    r.wout[z, ylo, k, yhi] = r.wo_asm[...].astype(BF16)
    for d in range(1, NZ):
        part = r.wout.at[z, ylo, k, yhi]
        sends.push(part, part, r.zo_s.at[d - 1], r.zo_r.at[d - 1], me.device(z=me.along_z(d)))

    @pl.when(me.moved)
    def _():
        swap_tok[0].wait_recv()
        norm_half(0)
        for n in (0, 1, 2):
            own_sends[n].start()
        swap_tok[1].wait_recv()
        norm_half(1)
        for n in (4, 3, 5):
            own_sends[n].start()

    def rows_of(dx, half):
        return r.normed.at[k * 4 + (x + dx) % 4, pl.ds(half * 128, 128)]

    def take(dx, half):
        part = rows_of(dx, half)
        arrived(part, r.ag_s.at[dx, half], r.ag_r.at[dx, half], me)
        sends.push(part, part, r.fw_s.at[dx, half], r.ag_r.at[4 + dx, half], me.sibling())

    take(3, 0)
    part = rows_of(3, 0)
    sends.push(part, part, r.ag_s.at[2, 0], r.ag_r.at[2, 0], right)
    take(1, 1)
    part = rows_of(1, 1)
    sends.push(part, part, r.ag_s.at[2, 1], r.ag_r.at[2, 1], left)

    for d in range(1, NZ):
        arrived(r.win.at[(z + NZ - d) % NZ, ylo, :, yhi], r.zi_s.at[d - 1], r.zi_r.at[d - 1], me)
    for d in range(1, 4):
        phi, plo = me.along_y(d)
        part = r.win.at[:, ylo, :, yhi]
        sends.push(part, part, r.yi_s.at[d - 1], r.yi_r.at[d - 1], me.device(ylo=plo, yhi=phi))

    @pl.when(me.moved)
    def _():
        swap_cot.start()

    take(3, 1)
    take(1, 0)
    for d in range(1, NZ):
        arrived(r.wout.at[(z + NZ - d) % NZ, ylo, k, yhi], r.zo_s.at[d - 1], r.zo_r.at[d - 1], me)
    for d in range(1, 4):
        phi, plo = me.along_y(d)
        part = r.wout.at[:, ylo, k, yhi]
        sends.push(part, part, r.yo_s.at[d - 1], r.yo_r.at[d - 1], me.device(ylo=plo, yhi=phi))
    arrived(r.len_recv, r.swap_s.at[3], r.swap_r.at[3], me)
    r.lens[...] = jnp.where(me.moved, r.len_recv[...], r.len_send[...])
    take(2, 0)
    take(2, 1)
    for d in range(1, 4):
        shi, slo = me.along_y(4 - d)
        arrived(r.win.at[:, slo, :, shi], r.yi_s.at[d - 1], r.yi_r.at[d - 1], me)

    @pl.loop(0, 4)
    def _(i):
        project(r, k * 4 + i)

    for dx in range(4):
        for half in range(2):
            arrived(
                r.normed.at[(1 - k) * 4 + (x + dx) % 4, pl.ds(half * 128, 128)],
                r.fw_s.at[dx, half], r.ag_r.at[4 + dx, half], me,
            )

    @pl.loop(0, 4)
    def _(i):
        project(r, (1 - k) * 4 + i)

    for i in range(4):
        attend(r, i, i)

    for d in range(1, 4):
        shi, slo = me.along_y(4 - d)
        arrived(r.wout.at[:, slo, k, shi], r.yo_s.at[d - 1], r.yo_r.at[d - 1], me)
    sends.push(r.wout.at[:, :, k], r.wout.at[:, :, k], r.core_s.at[0], r.core_r.at[0], me.sibling())

    @pl.loop(4, 8)
    def _(i):
        attend(r, i, 4)

    @pl.when(me.moved)
    def _():
        swap_cot.wait_recv()

    @pl.when(stays)
    def _():
        load_cot.wait()

    arrived(r.wout.at[:, :, 1 - k], r.core_s.at[0], r.core_r.at[0], me)

    @pl.loop(0, 4)
    def _(i):
        pair = dot(r.cotr[...], r.wout[pl.ds(2 * i, 2)].reshape(256, D), ABT)
        r.dsend[2 * i] = pair[:, :HD].astype(BF16)
        r.dsend[2 * i + 1] = pair[:, HD:].astype(BF16)

    r.dmix[w] = r.dsend[me.head]
    for d in range(1, 8):
        pk, px = me.row(d // 4, d % 4)
        sends.push(
            r.dsend.at[2 * px + pk], r.dmix.at[w], r.dm_s.at[d - 1], r.dm_r.at[d - 1], me.device(k=pk, x=px)
        )
    for d in range(1, 8):
        sk, sx = row_source(d)
        arrived(r.dmix.at[sk * 4 + sx], r.dm_s.at[d - 1], r.dm_r.at[d - 1], me)

    @pl.loop(0, 8)
    def _(i):
        row_stats(r, i)

    for d in range(1, 8):
        pk, px = me.row(d // 4, d % 4)
        sends.push(r.stats, r.every.at[w], r.st_s.at[d - 1], r.st_r.at[d - 1], me.device(k=pk, x=px))
    r.every[w] = r.stats[...]
    r.comb[...] = jnp.zeros_like(r.comb)
    r.dquery[...] = jnp.zeros_like(r.dquery)
    for d in range(1, 8):
        sk, sx = row_source(d)
        arrived(r.every.at[sk * 4 + sx], r.st_s.at[d - 1], r.st_r.at[d - 1], me)

    @pl.loop(0, 8)
    def _(i):
        gate_rows(r, i)

    r.mixed[me.head] = r.msend[w]
    for d in range(1, 8):
        pk, px = me.row(d // 4, d % 4)
        sends.push(
            r.msend.at[pk * 4 + px], r.mixed.at[me.head], r.mx_s.at[d - 1], r.mx_r.at[d - 1], me.device(k=pk, x=px)
        )

    @pl.loop(0, 3)
    def _(j):
        attend_back(r, j, 4)

    for d in range(1, 8):
        sk, sx = row_source(d)
        arrived(r.mixed.at[2 * sx + sk], r.mx_s.at[d - 1], r.mx_r.at[d - 1], me)

    @pl.loop(0, 4)
    def _(n):
        pair = jnp.concatenate([r.mixed[2 * n], r.mixed[2 * n + 1]], axis=1)
        product = dot(pair, r.cotr[...], ATB)
        r.ps[pl.ds(2 * n, 2)] = product.astype(BF16).reshape(2, 2, 2, 2, 16, D)

    sends.push(r.ps.at[:, :, 1 - k], r.pc, r.pc_s.at[0], r.pc_r.at[0], me.sibling())

    joined = jnp.concatenate([r.mixed[h] for h in range(HEADS)], axis=1)
    for n in range(4):
        cols = pl.ds(n * 256, 256)
        product = dot(joined, r.wout[:, :, :, :, :, cols].reshape(D, 256))
        r.lay[:, cols] = (product + r.tokr[:, cols].astype(F32)).astype(BF16)
    swap_lay = copy(r.lay, layer_out, r.sw_s.at[0], r.sw_r.at[0], me.partner())
    swap_grad = copy(r.grad, tok_grad, r.sw_s.at[1], r.sw_r.at[1], me.partner())

    @pl.when(stays)
    def _():
        layer_out[...] = r.lay[...]

    arrived(r.pc, r.pc_s.at[0], r.pc_r.at[0], me)

    @pl.loop(0, NZ)
    def _(n):
        r.pk_sum[n] = (r.ps[n, :, k].astype(F32) + r.pc[n].astype(F32)).astype(BF16)

    for d in range(1, 4):
        phi, plo = me.along_y(d)
        sends.push(
            r.pk_sum.at[:, plo, phi], r.py.at[d - 1], r.py_s.at[d - 1], r.py_r.at[d - 1], me.device(ylo=plo, yhi=phi)
        )

    @pl.when(me.moved)
    def _():
        swap_lay.start()

    @pl.loop(3, 4)
    def _(j):
        attend_back(r, j, 4)

    for j in range(4, 8):
        attend_back(r, j, 7 - j)

    @pl.loop(0, 8)
    def _(i):
        r.dhidden[i, :, 256:384] = (r.dquery[i] * HALF_FACTOR * r.slope[i, :, 256:384].astype(F32)).astype(BF16)

    def back_product(block, n):
        return dot(r.dhidden[block], r.win[pl.ds(2 * n, 2)].reshape(256, 512), ABT)

    def partial(dx):
        there = (1 - k) * 4 + (x + dx) % 4
        here = k * 4 + (x + dx) % 4

        @pl.loop(0, 4)
        def _(n):
            cols = pl.ds(pl.multiple_of(n * 256, 256), 256)
            r.es_send[dx, :, cols] = back_product(there, n).astype(BF16)

        sends.push(r.es_send.at[dx], r.es_recv.at[dx], r.sib_s.at[dx], r.sib_r.at[dx], me.sibling())

        @pl.loop(0, 4)
        def _(n):
            cols = pl.ds(pl.multiple_of(n * 256, 256), 256)
            r.esum[dx, :, cols] = back_product(here, n)

    def from_sibling(dx):
        arrived(r.es_recv.at[dx], r.sib_s.at[dx], r.sib_r.at[dx], me)

    def to_neighbour(side, half, extra):
        part = pl.ds(half * 128, 128)
        dx = 1 + 2 * side
        total = r.esum[dx, part] + r.es_recv[dx, part].astype(F32)
        if extra is not None:
            total = total + extra.astype(F32)
        r.nb_send[side, part] = total.astype(BF16)
        sends.push(
            r.nb_send.at[side, part], r.nb_recv.at[side, part],
            r.nb_s.at[side, half], r.nb_r.at[side, half], (right, left)[side],
        )

    partial(2)
    partial(1)
    from_sibling(2)
    r.x2_send[...] = (r.esum[2] + r.es_recv[2].astype(F32)).astype(BF16)
    sends.push(r.x2_send.at[pl.ds(0, 128)], r.rl_recv.at[0], r.rl_s.at[0], r.rl_r.at[0], right)
    sends.push(r.x2_send.at[pl.ds(128, 128)], r.rl_recv.at[1], r.rl_s.at[1], r.rl_r.at[1], left)
    partial(3)
    from_sibling(1)
    to_neighbour(0, 1, None)
    from_sibling(3)
    to_neighbour(1, 0, None)

    @pl.loop(0, 4)
    def _(n):
        cols = pl.ds(pl.multiple_of(n * 256, 256), 256)
        product = dot(r.normed[:, :, cols].reshape(8 * ROWS, 256), r.dhidden[...].reshape(8 * ROWS, 512), ATB)
        r.gs[pl.ds(2 * n, 2)] = product.astype(BF16).reshape(2, 2, 2, 2, 16, 512)

    for d in range(1, 4):
        phi, plo = me.along_y(d)
        sends.push(
            r.gs.at[:, plo, :, phi], r.gy.at[d - 1], r.gy_s.at[d - 1], r.gy_r.at[d - 1], me.device(ylo=plo, yhi=phi)
        )

    for side in range(2):
        arrived(r.rl_recv.at[side], r.rl_s.at[side], r.rl_r.at[side], me)
        to_neighbour(side, side, r.rl_recv[side])
    partial(0)

    for d in range(1, 4):
        arrived(r.py.at[d - 1], r.py_s.at[d - 1], r.py_r.at[d - 1], me)

    @pl.loop(0, NZ)
    def _(n):
        total = r.pk_sum[n, ylo, yhi].astype(F32)
        for d in range(3):
            total = total + r.py[d, n].astype(F32)
        r.pz_send[n] = total.astype(BF16)

    for d in range(1, NZ):
        to = me.along_z(d)
        sends.push(r.pz_send.at[to], r.pz.at[d - 1], r.pz_s.at[d - 1], r.pz_r.at[d - 1], me.device(z=to))

    for d in range(1, 4):
        arrived(r.gy.at[d - 1], r.gy_s.at[d - 1], r.gy_r.at[d - 1], me)

    @pl.loop(0, NZ)
    def _(n):
        total = r.gs[n, ylo, :, yhi].astype(F32)
        for d in range(3):
            total = total + r.gy[d, n].astype(F32)
        r.gz_send[n] = total.astype(BF16)

    for d in range(1, NZ):
        to = me.along_z(d)
        sends.push(r.gz_send.at[to], r.gz.at[d - 1], r.gz_s.at[d - 1], r.gz_r.at[d - 1], me.device(z=to))

    from_sibling(0)
    for side, half in ((0, 1), (1, 0), (0, 0), (1, 1)):
        arrived(r.nb_recv.at[side, pl.ds(half * 128, 128)], r.nb_s.at[side, half], r.nb_r.at[side, half], me)

    @pl.loop(0, 4)
    def _(n):
        part = pl.ds(pl.multiple_of(n * 64, 64), 64)
        upstream = (
            r.esum[0, part]
            + r.es_recv[0, part].astype(F32)
            + r.nb_recv[0, part].astype(F32)
            + r.nb_recv[1, part].astype(F32)
        )
        normal, inverse = normalize(r.tokr[part].astype(F32))
        first = jnp.mean(upstream, axis=-1, keepdims=True)
        second = jnp.mean(upstream * normal, axis=-1, keepdims=True)
        r.grad[part] = (inverse * (upstream - first - normal * second) + r.cotr[part].astype(F32)).astype(BF16)

    @pl.when(me.moved)
    def _():
        swap_grad.start()

    @pl.when(stays)
    def _():
        tok_grad[...] = r.grad[...]

    for d in range(1, NZ):
        arrived(r.pz.at[d - 1], r.pz_s.at[d - 1], r.pz_r.at[d - 1], me)
    total = r.pz_send[z].astype(F32)
    for d in range(1, NZ):
        total = total + r.pz[d - 1].astype(F32)
    for px in range(4):
        for b in range(8):
            r.px_f[px, b * 4 : b * 4 + 4, :] = total[px * 4 : px * 4 + 4, b * HD : (b + 1) * HD]
    r.px_recv[x] = r.px_f[x]
    for d in range(1, 4):
        pk, px = me.row(0, d)
        sends.push(r.px_f.at[px], r.px_recv.at[x], r.px_s.at[d - 1], r.px_r.at[d - 1], me.device(x=px))

    for d in range(1, NZ):
        arrived(r.gz.at[d - 1], r.gz_s.at[d - 1], r.gz_r.at[d - 1], me)
    total = r.gz_send[z].astype(F32)
    for d in range(1, NZ):
        total = total + r.gz[d - 1].astype(F32)
    for c in range(2):
        for px in range(4):
            for b in range(4):
                r.gx_f[c * 4 + px, b * 4 : b * 4 + 4, :] = total[c, px * 4 : px * 4 + 4, b * HD : (b + 1) * HD]
    r.gx_recv[w] = r.gx_f[w]
    for d in range(1, 8):
        pk, px = me.row(d // 4, d % 4)
        sends.push(
            r.gx_f.at[pk * 4 + px], r.gx_recv.at[w], r.gx_s.at[d - 1], r.gx_r.at[d - 1], me.device(k=pk, x=px)
        )

    for d in range(1, 4):
        arrived(r.px_recv.at[(x + 4 - d) % 4], r.px_s.at[d - 1], r.px_r.at[d - 1], me)
    total = r.px_recv[0] + r.px_recv[1] + r.px_recv[2] + r.px_recv[3]
    for b in range(8):
        wo_grad[:, b * HD : (b + 1) * HD] = total[b * 4 : b * 4 + 4]
    for d in range(1, 8):
        sk, sx = row_source(d)
        arrived(r.gx_recv.at[sk * 4 + sx], r.gx_s.at[d - 1], r.gx_r.at[d - 1], me)
    for src in range(8):
        h = 2 * (src % 4) + src // 4
        for b in range(4):
            wi_grad[:, b * D + h * HD : b * D + (h + 1) * HD] = r.gx_recv[src, b * 4 : b * 4 + 4, :]
    sends.drain()
    for one in own_sends:
        one.wait_send()

    @pl.when(me.moved)
    def _():
        for one in swap_tok:
            one.wait_send()
        swap_cot.wait_send()
        swap_lay.wait()
        swap_grad.wait()


def local(tokens, lengths, in_weight, out_weight, cotangent):
    anywhere = pl.BlockSpec(memory_space=pl.ANY)
    shapes = [((ROWS, D), BF16), ((ROWS, D), BF16), ((4, 4 * D), F32), ((4, D), F32)]
    scratch = [pltpu.VMEM(shape, kind) for shape, kind in BUFFERS.values()]
    for shape in SEMAPHORES.values():
        scratch += [DMA(shape), DMA(shape)]
    return tuple(
        pl.pallas_call(
            kernel,
            out_shape=[jax.ShapeDtypeStruct(s, t) for s, t in shapes],
            in_specs=[anywhere, anywhere, VMEM, VMEM, VMEM],
            out_specs=[VMEM] * 4,
            scratch_shapes=scratch,
            compiler_params=pltpu.CompilerParams(
                collective_id=0, has_side_effects=True, vmem_limit_bytes=60 << 20
            ),
            name="layer",
        )(tokens, cotangent, in_weight, out_weight, lengths)
    )


def solution(mesh):
    both = P(("dp", "seq"), None)
    return jax.shard_map(
        local,
        mesh=mesh,
        in_specs=(both, P("dp", None), both, both, both),
        out_specs=(both, both, both, both),
        check_vma=False,
    )
```

time: 1960 us -> 142 us (0.07)
  waiting for transfers between devices: 1590 us -> 0 us
  matrix products: 142 us -> 0 us
  Pallas kernels: 0 us -> 137 us
  local copies, waits for them, and re-layouts: 113 us -> 4.11 us
  other arithmetic: 30.9 us -> 0 us
  blocking collectives: 30.3 us -> 0 us
    all_gather x2 -> x0, waiting for transfers between devices: 1350 us -> none  [the longest x1 721 us: local(): lax.all_gather(in_weight, ('dp', 'seq'), axis=0, tiled=True)]
    dot_general x66 -> x0, matrix products: 142 us -> none  [the longest x10 26.6 us: compute(): jnp.einsum('hqk,qhd->khd', weights, d_query, preferred_element_type=jnp.f...]
    pallas_call x0 -> x1, Pallas kernels: none -> 137 us  [local(): pl.pallas_call(kernel, out_shape=[jax.ShapeDtypeStruct(s, t) for s, t in...]
    reduce_scatter x2 -> x0, waiting for transfers between devices: 117 us -> none  [the longest x1 117 us: local(): lax.psum_scatter(in_partial.astype(jnp.bfloat16), 'dp', scatter_dimension...]
    unnamed x6 -> x0, waiting for transfers between devices: 89 us -> none
    all_to_all x3 -> x0, waiting for transfers between devices: 35.3 us -> none  [the longest x2 35.3 us: to_heads(): lax.all_to_all(stacked, 'seq', split_axis=2, concat_axis=0, tiled=True)]
    dynamic_slice x68 -> x0, local copies, waits for them, and re-layouts: 31.2 us -> none  [the longest x8 10.2 us: one_query(): query_rows = lax.dynamic_slice_in_dim(queries, q_start, block_rows, 0)]
    all_to_all x1 -> x0, blocking collectives: 30.3 us -> none  [to_tokens(): lax.all_to_all(stacked, 'seq', split_axis=0, concat_axis=2, tiled=True)]
  transfers between devices with their start and end apart: 8 -> 0, of which waited for: 6 -> 0; matrix products, arithmetic and copies ran while one was open for 12% -> 0% of each run, Pallas kernels for 0% -> 0%
where the time goes in v2:
time: 142 us
  Pallas kernels  137 us (96%)
  local copies, waits for them, and re-layouts  4.11 us (3%)
    pallas_call x1, Pallas kernels, local(): pl.pallas_call(kernel, out_shape=[jax.ShapeDtypeStruct(s, t) for s, t in...  137 us
    unnamed x10, local copies, waits for them, and re-layouts  4.11 us

profile of v2, /device:TPU:1, one launch (start us, length us, event | category | flops | bytes accessed | tf_op | source)
XLA Modules:
  0.0 142.1 jit_solution(8258716511228266863)
XLA Ops:
  0.6 137.4 %layer.1 = (bf16[256,1024]{1,0:T(8,128)(2,1)}, bf16[256,1024]{1,0:T(8,128)(2,1)}, f32[4,4096]{1,0:T(4,128)}, f32[4,1024]{1,0:T(4,128)}) custom-call(bf16[256,1024]{1,0:T(8,128)(2,1)} %tok.1, bf16[256,1024]{1,0:T(8,128)(2,1)} %cot.1, bf16[4,4096]{1,0:T(4,128)(2,1)} %wi.1, bf16[4,1024]{1,0:T(4,128)(2,1)} %wo.1, s32[1,4]{1,0:T(1,128)} %lengths.1), custom_call_target="tpu_custom_call" | custom-call | tf_op jit(solution)/shard_map/layer/pallas_call | solution.py:735
  138.0 0.0 copy-start
  138.0 1.9 %copy.13 = bf16[256,1024]{1,0:T(8,128)(2,1)} copy(bf16[256,1024]{1,0:T(8,128)(2,1)} %get-tuple-element.8) | data formatting | bytes 1048576
  139.9 0.0 copy-done
  139.9 0.0 copy-start.1
  139.9 0.8 copy.14
  140.7 0.1 copy-done.1
  140.8 0.0 copy-start.2
  140.8 0.6 copy.15
  141.4 0.1 copy-done.2
  141.5 0.6 copy.16
Async XLA Ops:
  138.0 1.9 %copy-start = (bf16[256,1024]{1,0:T(8,128)(2,1)S(1)}, bf16[256,1024]{1,0:T(8,128)(2,1)}, u32[]{:S(2)}) copy-start(bf16[256,1024]{1,0:T(8,128)(2,1)} %get-tuple-element.9) | copy-start | bytes 1572868
  139.9 0.9 copy-start.1
  140.8 0.7 copy-start.2

commit v3 on v2

--- a/solution.py
+++ b/solution.py
@@ -77,20 +77,17 @@
         return peers
 
 
-def greet(me, peers, with_partner):
+def greet(me, peers, meanwhile):
     barrier = pltpu.get_barrier_semaphore()
     for peer in peers:
         pl.semaphore_signal(barrier, inc=1, device_id=peer, device_id_type=MESH)
-    if with_partner:
-
-        @pl.when(me.moved)
-        def _():
-            pl.semaphore_signal(barrier, inc=1, device_id=me.partner(), device_id_type=MESH)
-
-    if with_partner:
-        pl.semaphore_wait(barrier, len(peers) + me.moved.astype(jnp.int32))
-    else:
-        pl.semaphore_wait(barrier, len(peers))
+
+    @pl.when(me.moved)
+    def _():
+        pl.semaphore_signal(barrier, inc=1, device_id=me.partner(), device_id_type=MESH)
+
+    meanwhile()
+    pl.semaphore_wait(barrier, len(peers) + me.moved.astype(jnp.int32))
 
 
 def copy(src, dst, send, recv, to):
@@ -138,28 +135,33 @@
     "len_send": ((8, 128), jnp.int32), "len_recv": ((8, 128), jnp.int32), "lens": ((8, 128), jnp.int32),
     "wi_f": ((8, 16, 128), F32), "wi_send": ((8, 16, 128), BF16), "wi_recv": ((8, 16, 128), BF16),
     "wi_asm": ((2, 16, 512), F32),
-    "wo_f": ((32, 128), F32), "wo_send": ((32, 128), BF16), "wo_recv": ((4, 32, 128), BF16), "wo_asm": ((16, D), F32),
-    "win": ((NZ, 2, 2, 2, 16, 512), BF16), "wout": ((NZ, 2, 2, 2, 16, D), BF16),
+    "wo_f": ((4, 16, 128), F32), "wo_send": ((4, 16, 128), BF16), "wo_recv": ((4, 16, 128), BF16),
+    "wo_asm": ((16, 256), F32),
+    "win": ((NZ, 2, 2, 2, 16, 512), BF16), "wout": ((4, NZ, 2, 2, 2, 16, 256), BF16),
     "normed": ((8, ROWS, D), BF16), "gated": ((8, ROWS, 512), BF16), "slope": ((8, ROWS, 512), BF16),
     "dsend": ((8, ROWS, HD), BF16), "dmix": ((8, ROWS, HD), BF16),
-    "attn": ((8, ROWS, HD), BF16), "stats": ((8, 8, ROWS), F32), "every": ((8, 8, 8, ROWS), F32),
+    "attn": ((8, ROWS, HD), BF16), "stats": ((4, 8, ROWS), F32), "every": ((8, 4, 8, ROWS), F32),
     "comb": ((128, ROWS), F32), "msend": ((8, ROWS, HD), BF16), "mixed": ((8, ROWS, HD), BF16),
     "dattn": ((8, ROWS, HD), BF16), "dhidden": ((8, ROWS, 512), BF16), "dquery": ((8, ROWS, HD), F32),
     "lay": ((ROWS, D), BF16), "grad": ((ROWS, D), BF16),
     "esum": ((4, ROWS, D), F32), "es_send": ((4, ROWS, D), BF16), "es_recv": ((4, ROWS, D), BF16),
     "x2_send": ((ROWS, D), BF16), "rl_recv": ((2, 128, D), BF16),
     "nb_send": ((2, ROWS, D), BF16), "nb_recv": ((2, ROWS, D), BF16),
-    "gs": ((NZ, 2, 2, 2, 16, 512), BF16), "gy": ((3, NZ, 2, 16, 512), BF16),
-    "gz_send": ((NZ, 2, 16, 512), BF16), "gz": ((7, 2, 16, 512), BF16),
+    "gs": ((NZ, 2, 2, 2, 16, 512), BF16),
+    "gy": ((3, NZ, 16, 512), BF16), "gz_send": ((NZ, 16, 512), BF16), "gz": ((7, 16, 512), BF16),
+    "hz": ((7, 2, 2, 16, 512), BF16), "hy_send": ((2, 2, 16, 512), BF16), "hy": ((3, 16, 512), BF16),
     "gx_f": ((8, 16, 128), F32), "gx_recv": ((8, 16, 128), F32),
-    "ps": ((NZ, 2, 2, 2, 16, D), BF16), "pc": ((NZ, 2, 2, 16, D), BF16), "pk_sum": ((NZ, 2, 2, 16, D), BF16),
-    "py": ((3, NZ, 16, D), BF16), "pz_send": ((NZ, 16, D), BF16), "pz": ((7, 16, D), BF16),
-    "px_f": ((4, 32, 128), F32), "px_recv": ((4, 32, 128), F32),
+    "ps": ((4, NZ, 2, 2, 2, 16, 256), BF16), "pc": ((4, NZ, 2, 2, 16, 256), BF16),
+    "pk_sum": ((4, NZ, 2, 2, 16, 256), BF16), "pq": ((3, NZ, 2, 2, 16, 256), BF16), "pq_sum": ((NZ, 2, 2, 16, 256), BF16),
+    "py": ((3, NZ, 16, 256), BF16), "pz_send": ((NZ, 16, 256), BF16), "pz": ((7, 16, 256), BF16),
+    "px_f": ((4, 8, 128), F32), "px_recv": ((4, 8, 128), F32),
 }
 SEMAPHORES = {
-    "load": (2,), "swap": (4,), "xi": (7,), "xo": (3,), "zi": (7,), "zo": (7,), "yi": (3,), "yo": (3,), "core": (1,),
+    "load": (2,), "swap": (4,), "xi": (7,), "xo": (3,), "zi": (7,), "zo": (7,), "yi": (3,), "yo": (3,), "xq": (3,), "core": (4,),
+    "zj": (7,), "yj": (3,),
     "ag": (8, 2), "fw": (4, 2), "dm": (7,), "st": (7,), "mx": (7,), "sib": (4,), "rl": (2,), "nb": (2, 2),
-    "gy": (3,), "gz": (7,), "gx": (7,), "pc": (1,), "py": (3,), "pz": (7,), "px": (3,), "sw": (2,),
+    "gy": (3,), "gz": (7,), "hy": (3,), "hz": (7,), "gx": (7,),
+    "pc": (1,), "pq": (3,), "py": (3,), "pz": (7,), "px": (3,), "sw": (3,),
 }
 
 
@@ -201,7 +203,8 @@
     r.attn[i] = total.astype(BF16)
 
 
-def row_stats(r, i):
+def row_stats(r, pair, side):
+    i = 2 * pair + side
     value = r.attn[i].astype(F32)
     upstream = r.dmix[i].astype(F32) * r.gated[i, :, 0:128].astype(F32)
     mean = jnp.mean(value, axis=-1, keepdims=True)
@@ -216,11 +219,12 @@
     packed = jnp.zeros((ROWS, HD), F32)
     for n, part in enumerate(parts):
         packed = jnp.where(lane == n, part, packed)
-    r.stats[i] = packed.T[0:8]
-
-
-def gate_rows(r, i):
-    mean, second, total, cross = (r.every[:, i, n, :] for n in range(4))
+    r.stats[pair, 4 * side : 4 * side + 4] = packed.T[0:4]
+
+
+def gate_rows(r, pair, side):
+    i = 2 * pair + side
+    mean, second, total, cross = (r.every[:, pair, 4 * side + n, :] for n in range(4))
     middle = jnp.mean(mean, axis=0, keepdims=True)
     apart = mean - middle
     variance = jnp.sum(second + HD * apart * apart, axis=0, keepdims=True) / D
@@ -287,7 +291,21 @@
         load_tok.start()
         load_cot.start()
 
-    greet(me, me.row_peers() + me.zy_peers(), True)
+    def prepare():
+        wide = wi[...].astype(F32)
+        for h in range(HEADS):
+            for b in range(4):
+                r.wi_f[h, b * 4 : b * 4 + 4, :] = wide[:, b * D + h * HD : b * D + (h + 1) * HD]
+        r.wi_send[...] = r.wi_f[...].astype(BF16)
+        wide_o = wo[...].astype(F32)
+        r.wo_f[...] = jnp.zeros_like(r.wo_f)
+        for b in range(8):
+            r.wo_f[b // 2, (b % 2) * 4 : (b % 2) * 4 + 4, :] = wide_o[:, b * HD : (b + 1) * HD]
+        r.wo_send[...] = r.wo_f[...].astype(BF16)
+        r.len_send[...] = jnp.zeros_like(r.len_send)
+        r.len_send[0:1, 0:4] = lengths[...]
+
+    greet(me, me.row_peers() + me.zy_peers(), prepare)
 
     swap_tok = [
         copy(tok.at[part], r.tokr.at[part], r.swap_s.at[n], r.swap_r.at[n], me.partner())
@@ -295,32 +313,22 @@
     ]
     swap_cot = copy(cot, r.cotr, r.swap_s.at[2], r.swap_r.at[2], me.partner())
 
-    @pl.when(me.moved)
-    def _():
-        swap_tok[0].start()
-        swap_tok[1].start()
-
-    wide = wi[...].astype(F32)
-    for h in range(HEADS):
-        for b in range(4):
-            r.wi_f[h, b * 4 : b * 4 + 4, :] = wide[:, b * D + h * HD : b * D + (h + 1) * HD]
-    r.wi_send[...] = r.wi_f[...].astype(BF16)
     for d in range(1, 8):
         pk, px = me.row(d // 4, d % 4)
         sends.push(
             r.wi_send.at[2 * px + pk], r.wi_recv.at[w], r.xi_s.at[d - 1], r.xi_r.at[d - 1], me.device(k=pk, x=px)
         )
     r.wi_recv[w] = r.wi_send[me.head]
-    wide_o = wo[...].astype(F32)
-    for b in range(8):
-        r.wo_f[b * 4 : b * 4 + 4, :] = wide_o[:, b * HD : (b + 1) * HD]
-    r.wo_send[...] = r.wo_f[...].astype(BF16)
     for d in range(1, 4):
         pk, px = me.row(0, d)
-        sends.push(r.wo_send, r.wo_recv.at[x], r.xo_s.at[d - 1], r.xo_r.at[d - 1], me.device(x=px))
-    r.wo_recv[x] = r.wo_send[...]
-    r.len_send[...] = jnp.zeros_like(r.len_send)
-    r.len_send[0:1, 0:4] = lengths[...]
+        sends.push(r.wo_send.at[px], r.wo_recv.at[x], r.xo_s.at[d - 1], r.xo_r.at[d - 1], me.device(x=px))
+    r.wo_recv[x] = r.wo_send[x]
+
+    @pl.when(me.moved)
+    def _():
+        swap_tok[0].start()
+        swap_tok[1].start()
+
     sends.push(r.len_send, r.len_recv, r.swap_s.at[3], r.swap_r.at[3], me.sibling())
 
     def norm_half(half):
@@ -335,6 +343,32 @@
         own_sends.append(copy(own(half), own(half), r.ag_s.at[3, half], r.ag_r.at[3, half], right))
         own_sends.append(copy(own(half), own(half), r.ag_s.at[1, half], r.ag_r.at[1, half], left))
         own_sends.append(copy(own(half), own(half), r.fw_s.at[0, half], r.ag_r.at[4, half], me.sibling()))
+
+    def rows_of(dx, half):
+        return r.normed.at[k * 4 + (x + dx) % 4, pl.ds(half * 128, 128)]
+
+    def onward(dx, half, sem, recv, to):
+        return copy(rows_of(dx, half), rows_of(dx, half), sem, recv, to)
+
+    first_sends = [
+        onward(3, 0, r.ag_s.at[2, 0], r.ag_r.at[2, 0], right),
+        onward(3, 0, r.fw_s.at[3, 0], r.ag_r.at[7, 0], me.sibling()),
+        onward(1, 1, r.ag_s.at[2, 1], r.ag_r.at[2, 1], left),
+        onward(1, 1, r.fw_s.at[1, 1], r.ag_r.at[5, 1], me.sibling()),
+    ]
+
+    def take_first():
+        arrived(rows_of(3, 0), r.ag_s.at[3, 0], r.ag_r.at[3, 0], me)
+        first_sends[0].start()
+        first_sends[1].start()
+        arrived(rows_of(1, 1), r.ag_s.at[1, 1], r.ag_r.at[1, 1], me)
+        first_sends[2].start()
+        first_sends[3].start()
+
+    def take(dx, half):
+        part = rows_of(dx, half)
+        arrived(part, r.ag_s.at[dx, half], r.ag_r.at[dx, half], me)
+        sends.push(part, part, r.fw_s.at[dx, half], r.ag_r.at[4 + dx, half], me.sibling())
 
     @pl.when(stays)
     def _():
@@ -353,20 +387,28 @@
             r.wi_asm[src // 4, (src % 4) * 4 : (src % 4) * 4 + 4, b * HD : (b + 1) * HD] = piece[b * 4 : b * 4 + 4]
     for c in range(2):
         r.win[z, ylo, c, yhi] = r.wi_asm[c].astype(BF16)
-    for d in range(1, NZ):
-        part = r.win.at[z, ylo, :, yhi]
+    for d in range(1, 4):
+        phi, plo = me.along_y(d)
+        part = r.win.at[z, ylo, 1, yhi]
+        sends.push(part, part, r.yj_s.at[d - 1], r.yj_r.at[d - 1], me.device(ylo=plo, yhi=phi))
+    for d in range(1, NZ):
+        part = r.win.at[z, ylo, 0, yhi]
         sends.push(part, part, r.zi_s.at[d - 1], r.zi_r.at[d - 1], me.device(z=me.along_z(d)))
 
     for d in range(1, 4):
         arrived(r.wo_recv.at[(x + 4 - d) % 4], r.xo_s.at[d - 1], r.xo_r.at[d - 1], me)
     for src in range(4):
         piece = r.wo_recv[src].astype(F32)
-        for b in range(8):
+        for b in range(2):
             r.wo_asm[src * 4 : src * 4 + 4, b * HD : (b + 1) * HD] = piece[b * 4 : b * 4 + 4]
-    r.wout[z, ylo, k, yhi] = r.wo_asm[...].astype(BF16)
-    for d in range(1, NZ):
-        part = r.wout.at[z, ylo, k, yhi]
+    r.wout[x, z, ylo, k, yhi] = r.wo_asm[...].astype(BF16)
+    for d in range(1, NZ):
+        part = r.wout.at[x, z, ylo, k, yhi]
         sends.push(part, part, r.zo_s.at[d - 1], r.zo_r.at[d - 1], me.device(z=me.along_z(d)))
+
+    @pl.when(stays)
+    def _():
+        take_first()
 
     @pl.when(me.moved)
     def _():
@@ -379,47 +421,51 @@
         for n in (4, 3, 5):
             own_sends[n].start()
 
-    def rows_of(dx, half):
-        return r.normed.at[k * 4 + (x + dx) % 4, pl.ds(half * 128, 128)]
-
-    def take(dx, half):
-        part = rows_of(dx, half)
-        arrived(part, r.ag_s.at[dx, half], r.ag_r.at[dx, half], me)
-        sends.push(part, part, r.fw_s.at[dx, half], r.ag_r.at[4 + dx, half], me.sibling())
-
-    take(3, 0)
-    part = rows_of(3, 0)
-    sends.push(part, part, r.ag_s.at[2, 0], r.ag_r.at[2, 0], right)
-    take(1, 1)
-    part = rows_of(1, 1)
-    sends.push(part, part, r.ag_s.at[2, 1], r.ag_r.at[2, 1], left)
-
-    for d in range(1, NZ):
-        arrived(r.win.at[(z + NZ - d) % NZ, ylo, :, yhi], r.zi_s.at[d - 1], r.zi_r.at[d - 1], me)
+    for d in range(1, 4):
+        shi, slo = me.along_y(4 - d)
+        arrived(r.win.at[z, slo, 1, shi], r.yj_s.at[d - 1], r.yj_r.at[d - 1], me)
+    for d in range(1, NZ):
+        part = r.win.at[z, :, 1, :]
+        sends.push(part, part, r.zj_s.at[d - 1], r.zj_r.at[d - 1], me.device(z=me.along_z(d)))
+
+    for d in range(1, NZ):
+        arrived(r.win.at[(z + NZ - d) % NZ, ylo, 0, yhi], r.zi_s.at[d - 1], r.zi_r.at[d - 1], me)
     for d in range(1, 4):
         phi, plo = me.along_y(d)
-        part = r.win.at[:, ylo, :, yhi]
+        part = r.win.at[:, ylo, 0, yhi]
         sends.push(part, part, r.yi_s.at[d - 1], r.yi_r.at[d - 1], me.device(ylo=plo, yhi=phi))
 
+    for d in range(1, NZ):
+        arrived(r.wout.at[x, (z + NZ - d) % NZ, ylo, k, yhi], r.zo_s.at[d - 1], r.zo_r.at[d - 1], me)
+    for d in range(1, 4):
+        phi, plo = me.along_y(d)
+        part = r.wout.at[x, :, ylo, k, yhi]
+        sends.push(part, part, r.yo_s.at[d - 1], r.yo_r.at[d - 1], me.device(ylo=plo, yhi=phi))
+
     @pl.when(me.moved)
     def _():
         swap_cot.start()
+        take_first()
 
     take(3, 1)
     take(1, 0)
-    for d in range(1, NZ):
-        arrived(r.wout.at[(z + NZ - d) % NZ, ylo, k, yhi], r.zo_s.at[d - 1], r.zo_r.at[d - 1], me)
-    for d in range(1, 4):
-        phi, plo = me.along_y(d)
-        part = r.wout.at[:, ylo, k, yhi]
-        sends.push(part, part, r.yo_s.at[d - 1], r.yo_r.at[d - 1], me.device(ylo=plo, yhi=phi))
+    take(2, 0)
+    take(2, 1)
+    for d in range(1, 4):
+        shi, slo = me.along_y(4 - d)
+        arrived(r.wout.at[x, :, slo, k, shi], r.yo_s.at[d - 1], r.yo_r.at[d - 1], me)
+    part = r.wout.at[x, :, :, k]
+    for d in range(1, 4):
+        pk, px = me.row(0, d)
+        sends.push(part, part, r.xq_s.at[d - 1], r.xq_r.at[d - 1], me.device(x=px))
+    sends.push(part, part, r.core_s.at[0], r.core_r.at[0], me.sibling())
     arrived(r.len_recv, r.swap_s.at[3], r.swap_r.at[3], me)
     r.lens[...] = jnp.where(me.moved, r.len_recv[...], r.len_send[...])
-    take(2, 0)
-    take(2, 1)
     for d in range(1, 4):
         shi, slo = me.along_y(4 - d)
-        arrived(r.win.at[:, slo, :, shi], r.yi_s.at[d - 1], r.yi_r.at[d - 1], me)
+        arrived(r.win.at[:, slo, 0, shi], r.yi_s.at[d - 1], r.yi_r.at[d - 1], me)
+    for d in range(1, NZ):
+        arrived(r.win.at[(z + NZ - d) % NZ, :, 1, :], r.zj_s.at[d - 1], r.zj_r.at[d - 1], me)
 
     @pl.loop(0, 4)
     def _(i):
@@ -440,9 +486,9 @@
         attend(r, i, i)
 
     for d in range(1, 4):
-        shi, slo = me.along_y(4 - d)
-        arrived(r.wout.at[:, slo, k, shi], r.yo_s.at[d - 1], r.yo_r.at[d - 1], me)
-    sends.push(r.wout.at[:, :, k], r.wout.at[:, :, k], r.core_s.at[0], r.core_r.at[0], me.sibling())
+        part = r.wout.at[(x + 4 - d) % 4, :, :, k]
+        arrived(part, r.xq_s.at[d - 1], r.xq_r.at[d - 1], me)
+        sends.push(part, part, r.core_s.at[d], r.core_r.at[d], me.sibling())
 
     @pl.loop(4, 8)
     def _(i):
@@ -456,11 +502,14 @@
     def _():
         load_cot.wait()
 
-    arrived(r.wout.at[:, :, 1 - k], r.core_s.at[0], r.core_r.at[0], me)
+    for d in range(4):
+        arrived(r.wout.at[(x + 4 - d) % 4, :, :, 1 - k], r.core_s.at[d], r.core_r.at[d], me)
 
     @pl.loop(0, 4)
     def _(i):
-        pair = dot(r.cotr[...], r.wout[pl.ds(2 * i, 2)].reshape(256, D), ABT)
+        pair = jnp.zeros((ROWS, 256), F32)
+        for q in range(4):
+            pair = pair + dot(r.cotr[:, q * 256 : (q + 1) * 256], r.wout[q, pl.ds(2 * i, 2)].reshape(256, 256), ABT)
         r.dsend[2 * i] = pair[:, :HD].astype(BF16)
         r.dsend[2 * i + 1] = pair[:, HD:].astype(BF16)
 
@@ -474,9 +523,10 @@
         sk, sx = row_source(d)
         arrived(r.dmix.at[sk * 4 + sx], r.dm_s.at[d - 1], r.dm_r.at[d - 1], me)
 
-    @pl.loop(0, 8)
-    def _(i):
-        row_stats(r, i)
+    @pl.loop(0, 4)
+    def _(pair):
+        row_stats(r, pair, 0)
+        row_stats(r, pair, 1)
 
     for d in range(1, 8):
         pk, px = me.row(d // 4, d % 4)
@@ -488,9 +538,10 @@
         sk, sx = row_source(d)
         arrived(r.every.at[sk * 4 + sx], r.st_s.at[d - 1], r.st_r.at[d - 1], me)
 
-    @pl.loop(0, 8)
-    def _(i):
-        gate_rows(r, i)
+    @pl.loop(0, 4)
+    def _(pair):
+        gate_rows(r, pair, 0)
+        gate_rows(r, pair, 1)
 
     r.mixed[me.head] = r.msend[w]
     for d in range(1, 8):
@@ -510,18 +561,22 @@
     @pl.loop(0, 4)
     def _(n):
         pair = jnp.concatenate([r.mixed[2 * n], r.mixed[2 * n + 1]], axis=1)
-        product = dot(pair, r.cotr[...], ATB)
-        r.ps[pl.ds(2 * n, 2)] = product.astype(BF16).reshape(2, 2, 2, 2, 16, D)
-
-    sends.push(r.ps.at[:, :, 1 - k], r.pc, r.pc_s.at[0], r.pc_r.at[0], me.sibling())
+        product = dot(pair, r.cotr[...], ATB).astype(BF16)
+        for q in range(4):
+            r.ps[q, pl.ds(2 * n, 2)] = product[:, q * 256 : (q + 1) * 256].reshape(2, 2, 2, 2, 16, 256)
+
+    sends.push(r.ps.at[:, :, :, 1 - k], r.pc, r.pc_s.at[0], r.pc_r.at[0], me.sibling())
 
     joined = jnp.concatenate([r.mixed[h] for h in range(HEADS)], axis=1)
     for n in range(4):
         cols = pl.ds(n * 256, 256)
-        product = dot(joined, r.wout[:, :, :, :, :, cols].reshape(D, 256))
+        product = dot(joined, r.wout[n].reshape(D, 256))
         r.lay[:, cols] = (product + r.tokr[:, cols].astype(F32)).astype(BF16)
     swap_lay = copy(r.lay, layer_out, r.sw_s.at[0], r.sw_r.at[0], me.partner())
-    swap_grad = copy(r.grad, tok_grad, r.sw_s.at[1], r.sw_r.at[1], me.partner())
+    swap_grad = [
+        copy(r.grad.at[part], tok_grad.at[part], r.sw_s.at[n], r.sw_r.at[n], me.partner())
+        for n, part in ((1, pl.ds(0, 128)), (2, pl.ds(128, 128)))
+    ]
 
     @pl.when(stays)
     def _():
@@ -531,13 +586,12 @@
 
     @pl.loop(0, NZ)
     def _(n):
-        r.pk_sum[n] = (r.ps[n, :, k].astype(F32) + r.pc[n].astype(F32)).astype(BF16)
-
-    for d in range(1, 4):
-        phi, plo = me.along_y(d)
-        sends.push(
-            r.pk_sum.at[:, plo, phi], r.py.at[d - 1], r.py_s.at[d - 1], r.py_r.at[d - 1], me.device(ylo=plo, yhi=phi)
-        )
+        for q in range(4):
+            r.pk_sum[q, n] = (r.ps[q, n, :, k].astype(F32) + r.pc[q, n].astype(F32)).astype(BF16)
+
+    for d in range(1, 4):
+        pk, px = me.row(0, d)
+        sends.push(r.pk_sum.at[px], r.pq.at[d - 1], r.pq_s.at[d - 1], r.pq_r.at[d - 1], me.device(x=px))
 
     @pl.when(me.moved)
     def _():
@@ -606,10 +660,29 @@
         product = dot(r.normed[:, :, cols].reshape(8 * ROWS, 256), r.dhidden[...].reshape(8 * ROWS, 512), ATB)
         r.gs[pl.ds(2 * n, 2)] = product.astype(BF16).reshape(2, 2, 2, 2, 16, 512)
 
+    for d in range(1, NZ):
+        to = me.along_z(d)
+        sends.push(r.gs.at[to, :, 1, :], r.hz.at[d - 1], r.hz_s.at[d - 1], r.hz_r.at[d - 1], me.device(z=to))
     for d in range(1, 4):
         phi, plo = me.along_y(d)
         sends.push(
-            r.gs.at[:, plo, :, phi], r.gy.at[d - 1], r.gy_s.at[d - 1], r.gy_r.at[d - 1], me.device(ylo=plo, yhi=phi)
+            r.gs.at[:, plo, 0, phi], r.gy.at[d - 1], r.gy_s.at[d - 1], r.gy_r.at[d - 1], me.device(ylo=plo, yhi=phi)
+        )
+
+    for d in range(1, 4):
+        arrived(r.pq.at[d - 1], r.pq_s.at[d - 1], r.pq_r.at[d - 1], me)
+
+    @pl.loop(0, NZ)
+    def _(n):
+        total = r.pk_sum[x, n].astype(F32)
+        for d in range(3):
+            total = total + r.pq[d, n].astype(F32)
+        r.pq_sum[n] = total.astype(BF16)
+
+    for d in range(1, 4):
+        phi, plo = me.along_y(d)
+        sends.push(
+            r.pq_sum.at[:, plo, phi], r.py.at[d - 1], r.py_s.at[d - 1], r.py_r.at[d - 1], me.device(ylo=plo, yhi=phi)
         )
 
     for side in range(2):
@@ -618,11 +691,37 @@
     partial(0)
 
     for d in range(1, 4):
-        arrived(r.py.at[d - 1], r.py_s.at[d - 1], r.py_r.at[d - 1], me)
+        arrived(r.gy.at[d - 1], r.gy_s.at[d - 1], r.gy_r.at[d - 1], me)
 
     @pl.loop(0, NZ)
     def _(n):
-        total = r.pk_sum[n, ylo, yhi].astype(F32)
+        total = r.gs[n, ylo, 0, yhi].astype(F32)
+        for d in range(3):
+            total = total + r.gy[d, n].astype(F32)
+        r.gz_send[n] = total.astype(BF16)
+
+    for d in range(1, NZ):
+        to = me.along_z(d)
+        sends.push(r.gz_send.at[to], r.gz.at[d - 1], r.gz_s.at[d - 1], r.gz_r.at[d - 1], me.device(z=to))
+    for d in range(1, NZ):
+        arrived(r.hz.at[d - 1], r.hz_s.at[d - 1], r.hz_r.at[d - 1], me)
+    for n in range(2):
+        total = r.gs[z, n, 1].astype(F32)
+        for d in range(7):
+            total = total + r.hz[d, n].astype(F32)
+        r.hy_send[n] = total.astype(BF16)
+    for d in range(1, 4):
+        phi, plo = me.along_y(d)
+        sends.push(
+            r.hy_send.at[plo, phi], r.hy.at[d - 1], r.hy_s.at[d - 1], r.hy_r.at[d - 1], me.device(ylo=plo, yhi=phi)
+        )
+
+    for d in range(1, 4):
+        arrived(r.py.at[d - 1], r.py_s.at[d - 1], r.py_r.at[d - 1], me)
+
+    @pl.loop(0, NZ)
+    def _(n):
+        total = r.pq_sum[n, ylo, yhi].astype(F32)
         for d in range(3):
             total = total + r.py[d, n].astype(F32)
         r.pz_send[n] = total.astype(BF16)
@@ -631,45 +730,35 @@
         to = me.along_z(d)
         sends.push(r.pz_send.at[to], r.pz.at[d - 1], r.pz_s.at[d - 1], r.pz_r.at[d - 1], me.device(z=to))
 
-    for d in range(1, 4):
-        arrived(r.gy.at[d - 1], r.gy_s.at[d - 1], r.gy_r.at[d - 1], me)
-
-    @pl.loop(0, NZ)
-    def _(n):
-        total = r.gs[n, ylo, :, yhi].astype(F32)
-        for d in range(3):
-            total = total + r.gy[d, n].astype(F32)
-        r.gz_send[n] = total.astype(BF16)
-
-    for d in range(1, NZ):
-        to = me.along_z(d)
-        sends.push(r.gz_send.at[to], r.gz.at[d - 1], r.gz_s.at[d - 1], r.gz_r.at[d - 1], me.device(z=to))
-
     from_sibling(0)
-    for side, half in ((0, 1), (1, 0), (0, 0), (1, 1)):
-        arrived(r.nb_recv.at[side, pl.ds(half * 128, 128)], r.nb_s.at[side, half], r.nb_r.at[side, half], me)
-
-    @pl.loop(0, 4)
-    def _(n):
-        part = pl.ds(pl.multiple_of(n * 64, 64), 64)
-        upstream = (
-            r.esum[0, part]
-            + r.es_recv[0, part].astype(F32)
-            + r.nb_recv[0, part].astype(F32)
-            + r.nb_recv[1, part].astype(F32)
-        )
-        normal, inverse = normalize(r.tokr[part].astype(F32))
-        first = jnp.mean(upstream, axis=-1, keepdims=True)
-        second = jnp.mean(upstream * normal, axis=-1, keepdims=True)
-        r.grad[part] = (inverse * (upstream - first - normal * second) + r.cotr[part].astype(F32)).astype(BF16)
-
-    @pl.when(me.moved)
-    def _():
-        swap_grad.start()
-
-    @pl.when(stays)
-    def _():
-        tok_grad[...] = r.grad[...]
+
+    def finish(half):
+        for side in range(2):
+            arrived(r.nb_recv.at[side, pl.ds(half * 128, 128)], r.nb_s.at[side, half], r.nb_r.at[side, half], me)
+        for n in range(2):
+            part = pl.ds(half * 128 + n * 64, 64)
+            upstream = (
+                r.esum[0, part]
+                + r.es_recv[0, part].astype(F32)
+                + r.nb_recv[0, part].astype(F32)
+                + r.nb_recv[1, part].astype(F32)
+            )
+            normal, inverse = normalize(r.tokr[part].astype(F32))
+            first = jnp.mean(upstream, axis=-1, keepdims=True)
+            second = jnp.mean(upstream * normal, axis=-1, keepdims=True)
+            r.grad[part] = (inverse * (upstream - first - normal * second) + r.cotr[part].astype(F32)).astype(BF16)
+
+        @pl.when(me.moved)
+        def _():
+            swap_grad[half].start()
+
+        @pl.when(stays)
+        def _():
+            part = pl.ds(half * 128, 128)
+            tok_grad[part] = r.grad[part]
+
+    finish(0)
+    finish(1)
 
     for d in range(1, NZ):
         arrived(r.pz.at[d - 1], r.pz_s.at[d - 1], r.pz_r.at[d - 1], me)
@@ -677,7 +766,7 @@
     for d in range(1, NZ):
         total = total + r.pz[d - 1].astype(F32)
     for px in range(4):
-        for b in range(8):
+        for b in range(2):
             r.px_f[px, b * 4 : b * 4 + 4, :] = total[px * 4 : px * 4 + 4, b * HD : (b + 1) * HD]
     r.px_recv[x] = r.px_f[x]
     for d in range(1, 4):
@@ -686,13 +775,20 @@
 
     for d in range(1, NZ):
         arrived(r.gz.at[d - 1], r.gz_s.at[d - 1], r.gz_r.at[d - 1], me)
+    for d in range(1, 4):
+        arrived(r.hy.at[d - 1], r.hy_s.at[d - 1], r.hy_r.at[d - 1], me)
     total = r.gz_send[z].astype(F32)
-    for d in range(1, NZ):
-        total = total + r.gz[d - 1].astype(F32)
+    for d in range(7):
+        total = total + r.gz[d].astype(F32)
+    other = r.hy_send[ylo, yhi].astype(F32)
+    for d in range(3):
+        other = other + r.hy[d].astype(F32)
     for c in range(2):
         for px in range(4):
             for b in range(4):
-                r.gx_f[c * 4 + px, b * 4 : b * 4 + 4, :] = total[c, px * 4 : px * 4 + 4, b * HD : (b + 1) * HD]
+                r.gx_f[c * 4 + px, b * 4 : b * 4 + 4, :] = (total, other)[c][
+                    px * 4 : px * 4 + 4, b * HD : (b + 1) * HD
+                ]
     r.gx_recv[w] = r.gx_f[w]
     for d in range(1, 8):
         pk, px = me.row(d // 4, d % 4)
@@ -702,9 +798,8 @@
 
     for d in range(1, 4):
         arrived(r.px_recv.at[(x + 4 - d) % 4], r.px_s.at[d - 1], r.px_r.at[d - 1], me)
-    total = r.px_recv[0] + r.px_recv[1] + r.px_recv[2] + r.px_recv[3]
     for b in range(8):
-        wo_grad[:, b * HD : (b + 1) * HD] = total[b * 4 : b * 4 + 4]
+        wo_grad[:, b * HD : (b + 1) * HD] = r.px_recv[b // 2, (b % 2) * 4 : (b % 2) * 4 + 4]
     for d in range(1, 8):
         sk, sx = row_source(d)
         arrived(r.gx_recv.at[sk * 4 + sx], r.gx_s.at[d - 1], r.gx_r.at[d - 1], me)
@@ -713,7 +808,7 @@
         for b in range(4):
             wi_grad[:, b * D + h * HD : b * D + (h + 1) * HD] = r.gx_recv[src, b * 4 : b * 4 + 4, :]
     sends.drain()
-    for one in own_sends:
+    for one in own_sends + first_sends:
         one.wait_send()
 
     @pl.when(me.moved)
@@ -722,7 +817,8 @@
             one.wait_send()
         swap_cot.wait_send()
         swap_lay.wait()
-        swap_grad.wait()
+        for one in swap_grad:
+            one.wait()
 
 
 def local(tokens, lengths, in_weight, out_weight, cotangent):

time: 142 us -> 130 us (0.915)
  Pallas kernels: 137 us -> 125 us
    pallas_call x1, Pallas kernels: 137 us -> 125 us  [local(): pl.pallas_call(kernel, out_shape=[jax.ShapeDtypeStruct(s, t) for s, t in...]
where the time goes in v3:
time: 130 us
  Pallas kernels  125 us (96%)
  local copies, waits for them, and re-layouts  4.11 us (3%)
    pallas_call x1, Pallas kernels, local(): pl.pallas_call(kernel, out_shape=[jax.ShapeDtypeStruct(s, t) for s, t in...  125 us
    unnamed x10, local copies, waits for them, and re-layouts  4.11 us

profile of v3, /device:TPU:1, one launch (start us, length us, event | category | flops | bytes accessed | tf_op | source)
XLA Modules:
  0.0 129.7 jit_solution(10359563212965044711)
XLA Ops:
  0.6 125.0 %layer.1 = (bf16[256,1024]{1,0:T(8,128)(2,1)}, bf16[256,1024]{1,0:T(8,128)(2,1)}, f32[4,4096]{1,0:T(4,128)}, f32[4,1024]{1,0:T(4,128)}) custom-call(bf16[256,1024]{1,0:T(8,128)(2,1)} %tok.1, bf16[256,1024]{1,0:T(8,128)(2,1)} %cot.1, bf16[4,4096]{1,0:T(4,128)(2,1)} %wi.1, bf16[4,1024]{1,0:T(4,128)(2,1)} %wo.1, s32[1,4]{1,0:T(1,128)} %lengths.1), custom_call_target="tpu_custom_call" | custom-call | tf_op jit(solution)/shard_map/layer/pallas_call | solution.py:831
  125.6 0.0 copy-start
  125.6 1.9 %copy.13 = bf16[256,1024]{1,0:T(8,128)(2,1)} copy(bf16[256,1024]{1,0:T(8,128)(2,1)} %get-tuple-element.8) | data formatting | bytes 1048576
  127.5 0.0 copy-done
  127.5 0.0 copy-start.1
  127.5 0.8 copy.14
  128.3 0.1 copy-done.1
  128.4 0.0 copy-start.2
  128.4 0.6 copy.15
  129.0 0.1 copy-done.2
  129.1 0.6 copy.16
Async XLA Ops:
  125.6 1.9 %copy-start = (bf16[256,1024]{1,0:T(8,128)(2,1)S(1)}, bf16[256,1024]{1,0:T(8,128)(2,1)}, u32[]{:S(2)}) copy-start(bf16[256,1024]{1,0:T(8,128)(2,1)} %get-tuple-element.9) | copy-start | bytes 1572868
  127.5 0.9 copy-start.1
  128.4 0.7 copy-start.2

commit v4 on v3

--- a/solution.py
+++ b/solution.py
@@ -135,9 +135,9 @@
     "len_send": ((8, 128), jnp.int32), "len_recv": ((8, 128), jnp.int32), "lens": ((8, 128), jnp.int32),
     "wi_f": ((8, 16, 128), F32), "wi_send": ((8, 16, 128), BF16), "wi_recv": ((8, 16, 128), BF16),
     "wi_asm": ((2, 16, 512), F32),
-    "wo_f": ((4, 16, 128), F32), "wo_send": ((4, 16, 128), BF16), "wo_recv": ((4, 16, 128), BF16),
-    "wo_asm": ((16, 256), F32),
-    "win": ((NZ, 2, 2, 2, 16, 512), BF16), "wout": ((4, NZ, 2, 2, 2, 16, 256), BF16),
+    "wo_f": ((2, 16, 128), F32), "wo_send": ((2, 16, 128), BF16), "wo_recv": ((4, 16, 128), BF16),
+    "wo_asm": ((2, 16, 256), F32),
+    "win": ((NZ, 2, 2, 2, 16, 512), BF16), "wout": ((2, 2, NZ, 2, 2, 2, 16, 256), BF16),
     "normed": ((8, ROWS, D), BF16), "gated": ((8, ROWS, 512), BF16), "slope": ((8, ROWS, 512), BF16),
     "dsend": ((8, ROWS, HD), BF16), "dmix": ((8, ROWS, HD), BF16),
     "attn": ((8, ROWS, HD), BF16), "stats": ((4, 8, ROWS), F32), "every": ((8, 4, 8, ROWS), F32),
@@ -151,17 +151,18 @@
     "gy": ((3, NZ, 16, 512), BF16), "gz_send": ((NZ, 16, 512), BF16), "gz": ((7, 16, 512), BF16),
     "hz": ((7, 2, 2, 16, 512), BF16), "hy_send": ((2, 2, 16, 512), BF16), "hy": ((3, 16, 512), BF16),
     "gx_f": ((8, 16, 128), F32), "gx_recv": ((8, 16, 128), F32),
-    "ps": ((4, NZ, 2, 2, 2, 16, 256), BF16), "pc": ((4, NZ, 2, 2, 16, 256), BF16),
-    "pk_sum": ((4, NZ, 2, 2, 16, 256), BF16), "pq": ((3, NZ, 2, 2, 16, 256), BF16), "pq_sum": ((NZ, 2, 2, 16, 256), BF16),
-    "py": ((3, NZ, 16, 256), BF16), "pz_send": ((NZ, 16, 256), BF16), "pz": ((7, 16, 256), BF16),
-    "px_f": ((4, 8, 128), F32), "px_recv": ((4, 8, 128), F32),
+    "ps": ((2, 2, NZ, 2, 2, 2, 16, 256), BF16), "pc": ((2, 2, NZ, 2, 2, 16, 256), BF16),
+    "pk_sum": ((2, 2, NZ, 2, 2, 16, 256), BF16), "pq": ((2, NZ, 2, 2, 16, 256), BF16),
+    "pq_sum": ((2, NZ, 2, 2, 16, 256), BF16),
+    "py": ((3, 2, NZ, 16, 256), BF16), "pz_send": ((NZ, 2, 16, 256), BF16), "pz": ((7, 2, 16, 256), BF16),
+    "px_f": ((4, 16, 128), F32), "px_recv": ((4, 16, 128), F32),
 }
 SEMAPHORES = {
-    "load": (2,), "swap": (4,), "xi": (7,), "xo": (3,), "zi": (7,), "zo": (7,), "yi": (3,), "yo": (3,), "xq": (3,), "core": (4,),
+    "load": (2,), "swap": (6,), "xi": (7,), "xo": (3,), "zi": (7,), "zo": (7,), "yi": (3,), "yo": (3,), "xq": (2,), "core": (3,),
     "zj": (7,), "yj": (3,),
-    "ag": (8, 2), "fw": (4, 2), "dm": (7,), "st": (7,), "mx": (7,), "sib": (4,), "rl": (2,), "nb": (2, 2),
+    "ag": (8, 4), "fw": (4, 4), "dm": (7,), "st": (7,), "mx": (7,), "sib": (4,), "rl": (2,), "nb": (2, 2),
     "gy": (3,), "gz": (7,), "hy": (3,), "hz": (7,), "gx": (7,),
-    "pc": (1,), "pq": (3,), "py": (3,), "pz": (7,), "px": (3,), "sw": (3,),
+    "pc": (1,), "pq": (2,), "py": (3,), "pz": (7,), "px": (3,), "sw": (3,),
 }
 
 
@@ -300,7 +301,7 @@
         wide_o = wo[...].astype(F32)
         r.wo_f[...] = jnp.zeros_like(r.wo_f)
         for b in range(8):
-            r.wo_f[b // 2, (b % 2) * 4 : (b % 2) * 4 + 4, :] = wide_o[:, b * HD : (b + 1) * HD]
+            r.wo_f[b // 2 % 2, (b // 4 * 2 + b % 2) * 4 : (b // 4 * 2 + b % 2) * 4 + 4, :] = wide_o[:, b * HD : (b + 1) * HD]
         r.wo_send[...] = r.wo_f[...].astype(BF16)
         r.len_send[...] = jnp.zeros_like(r.len_send)
         r.len_send[0:1, 0:4] = lengths[...]
@@ -309,9 +310,9 @@
 
     swap_tok = [
         copy(tok.at[part], r.tokr.at[part], r.swap_s.at[n], r.swap_r.at[n], me.partner())
-        for n, part in ((0, pl.ds(0, 128)), (1, pl.ds(128, 128)))
+        for n, part in ((n, pl.ds(n * 64, 64)) for n in range(4))
     ]
-    swap_cot = copy(cot, r.cotr, r.swap_s.at[2], r.swap_r.at[2], me.partner())
+    swap_cot = copy(cot, r.cotr, r.swap_s.at[4], r.swap_r.at[4], me.partner())
 
     for d in range(1, 8):
         pk, px = me.row(d // 4, d % 4)
@@ -321,62 +322,63 @@
     r.wi_recv[w] = r.wi_send[me.head]
     for d in range(1, 4):
         pk, px = me.row(0, d)
-        sends.push(r.wo_send.at[px], r.wo_recv.at[x], r.xo_s.at[d - 1], r.xo_r.at[d - 1], me.device(x=px))
-    r.wo_recv[x] = r.wo_send[x]
+        sends.push(r.wo_send.at[px % 2], r.wo_recv.at[x], r.xo_s.at[d - 1], r.xo_r.at[d - 1], me.device(x=px))
+    r.wo_recv[x] = r.wo_send[x % 2]
 
     @pl.when(me.moved)
     def _():
-        swap_tok[0].start()
-        swap_tok[1].start()
-
-    sends.push(r.len_send, r.len_recv, r.swap_s.at[3], r.swap_r.at[3], me.sibling())
-
-    def norm_half(half):
-        part = pl.ds(half * 128, 128)
+        for n in (0, 2, 1, 3):
+            swap_tok[n].start()
+
+    sends.push(r.len_send, r.len_recv, r.swap_s.at[5], r.swap_r.at[5], me.sibling())
+
+    def norm_chunk(n):
+        part = pl.ds(n * 64, 64)
         r.normed[w, part] = normalize(r.tokr[part].astype(F32))[0].astype(BF16)
 
-    def own(half):
-        return r.normed.at[w, pl.ds(half * 128, 128)]
-
-    own_sends = []
-    for half in range(2):
-        own_sends.append(copy(own(half), own(half), r.ag_s.at[3, half], r.ag_r.at[3, half], right))
-        own_sends.append(copy(own(half), own(half), r.ag_s.at[1, half], r.ag_r.at[1, half], left))
-        own_sends.append(copy(own(half), own(half), r.fw_s.at[0, half], r.ag_r.at[4, half], me.sibling()))
-
-    def rows_of(dx, half):
-        return r.normed.at[k * 4 + (x + dx) % 4, pl.ds(half * 128, 128)]
-
-    def onward(dx, half, sem, recv, to):
-        return copy(rows_of(dx, half), rows_of(dx, half), sem, recv, to)
-
-    first_sends = [
-        onward(3, 0, r.ag_s.at[2, 0], r.ag_r.at[2, 0], right),
-        onward(3, 0, r.fw_s.at[3, 0], r.ag_r.at[7, 0], me.sibling()),
-        onward(1, 1, r.ag_s.at[2, 1], r.ag_r.at[2, 1], left),
-        onward(1, 1, r.fw_s.at[1, 1], r.ag_r.at[5, 1], me.sibling()),
-    ]
+    def rows_of(dx, n):
+        return r.normed.at[k * 4 + (x + dx) % 4, pl.ds(n * 64, 64)]
+
+    def onward(dx, n, slot, to):
+        return copy(rows_of(dx, n), rows_of(dx, n), r.ag_s.at[slot, n], r.ag_r.at[slot, n], to)
+
+    def across(dx, n):
+        return copy(rows_of(dx, n), rows_of(dx, n), r.fw_s.at[dx, n], r.ag_r.at[4 + dx, n], me.sibling())
+
+    to_right = [onward(0, n, 3, right) for n in range(4)]
+    to_left = [onward(0, n, 1, left) for n in range(4)]
+    to_sibling = [across(0, n) for n in range(4)]
+    relay = {n: onward(3, n, 2, right) if n < 2 else onward(1, n, 2, left) for n in range(4)}
+    relay_sibling = {n: across(3 if n < 2 else 1, n) for n in range(4)}
+
+    def send_chunk(n):
+        (to_right if n < 2 else to_left)[n].start()
+        to_sibling[n].start()
+
+    def send_rest():
+        for n in (2, 3):
+            to_right[n].start()
+            to_left[n - 2].start()
 
     def take_first():
-        arrived(rows_of(3, 0), r.ag_s.at[3, 0], r.ag_r.at[3, 0], me)
-        first_sends[0].start()
-        first_sends[1].start()
-        arrived(rows_of(1, 1), r.ag_s.at[1, 1], r.ag_r.at[1, 1], me)
-        first_sends[2].start()
-        first_sends[3].start()
-
-    def take(dx, half):
-        part = rows_of(dx, half)
-        arrived(part, r.ag_s.at[dx, half], r.ag_r.at[dx, half], me)
-        sends.push(part, part, r.fw_s.at[dx, half], r.ag_r.at[4 + dx, half], me.sibling())
+        for n in (0, 2, 1, 3):
+            slot = 3 if n < 2 else 1
+            arrived(rows_of(slot, n), r.ag_s.at[slot, n], r.ag_r.at[slot, n], me)
+            relay[n].start()
+            relay_sibling[n].start()
+
+    def take(dx, n):
+        part = rows_of(dx, n)
+        arrived(part, r.ag_s.at[dx, n], r.ag_r.at[dx, n], me)
+        sends.push(part, part, r.fw_s.at[dx, n], r.ag_r.at[4 + dx, n], me.sibling())
 
     @pl.when(stays)
     def _():
         load_tok.wait()
-        norm_half(0)
-        norm_half(1)
-        for n in (0, 4, 3, 1, 2, 5):
-            own_sends[n].start()
+        for n in (0, 2, 1, 3):
+            norm_chunk(n)
+            send_chunk(n)
+        send_rest()
 
     for d in range(1, 8):
         sk, sx = row_source(d)
@@ -399,11 +401,12 @@
         arrived(r.wo_recv.at[(x + 4 - d) % 4], r.xo_s.at[d - 1], r.xo_r.at[d - 1], me)
     for src in range(4):
         piece = r.wo_recv[src].astype(F32)
-        for b in range(2):
-            r.wo_asm[src * 4 : src * 4 + 4, b * HD : (b + 1) * HD] = piece[b * 4 : b * 4 + 4]
-    r.wout[x, z, ylo, k, yhi] = r.wo_asm[...].astype(BF16)
-    for d in range(1, NZ):
-        part = r.wout.at[x, z, ylo, k, yhi]
+        for b in range(4):
+            r.wo_asm[b // 2, src * 4 : src * 4 + 4, b % 2 * HD : (b % 2 + 1) * HD] = piece[b * 4 : b * 4 + 4]
+    for n in range(2):
+        r.wout[x % 2, n, z, ylo, k, yhi] = r.wo_asm[n].astype(BF16)
+    for d in range(1, NZ):
+        part = r.wout.at[x % 2, :, z, ylo, k, yhi]
         sends.push(part, part, r.zo_s.at[d - 1], r.zo_r.at[d - 1], me.device(z=me.along_z(d)))
 
     @pl.when(stays)
@@ -412,14 +415,11 @@
 
     @pl.when(me.moved)
     def _():
-        swap_tok[0].wait_recv()
-        norm_half(0)
-        for n in (0, 1, 2):
-            own_sends[n].start()
-        swap_tok[1].wait_recv()
-        norm_half(1)
-        for n in (4, 3, 5):
-            own_sends[n].start()
+        for n in (0, 2, 1, 3):
+            swap_tok[n].wait_recv()
+            norm_chunk(n)
+            send_chunk(n)
+        send_rest()
 
     for d in range(1, 4):
         shi, slo = me.along_y(4 - d)
@@ -436,10 +436,10 @@
         sends.push(part, part, r.yi_s.at[d - 1], r.yi_r.at[d - 1], me.device(ylo=plo, yhi=phi))
 
     for d in range(1, NZ):
-        arrived(r.wout.at[x, (z + NZ - d) % NZ, ylo, k, yhi], r.zo_s.at[d - 1], r.zo_r.at[d - 1], me)
+        arrived(r.wout.at[x % 2, :, (z + NZ - d) % NZ, ylo, k, yhi], r.zo_s.at[d - 1], r.zo_r.at[d - 1], me)
     for d in range(1, 4):
         phi, plo = me.along_y(d)
-        part = r.wout.at[x, :, ylo, k, yhi]
+        part = r.wout.at[x % 2, :, :, ylo, k, yhi]
         sends.push(part, part, r.yo_s.at[d - 1], r.yo_r.at[d - 1], me.device(ylo=plo, yhi=phi))
 
     @pl.when(me.moved)
@@ -447,19 +447,9 @@
         swap_cot.start()
         take_first()
 
-    take(3, 1)
-    take(1, 0)
-    take(2, 0)
-    take(2, 1)
-    for d in range(1, 4):
-        shi, slo = me.along_y(4 - d)
-        arrived(r.wout.at[x, :, slo, k, shi], r.yo_s.at[d - 1], r.yo_r.at[d - 1], me)
-    part = r.wout.at[x, :, :, k]
-    for d in range(1, 4):
-        pk, px = me.row(0, d)
-        sends.push(part, part, r.xq_s.at[d - 1], r.xq_r.at[d - 1], me.device(x=px))
-    sends.push(part, part, r.core_s.at[0], r.core_r.at[0], me.sibling())
-    arrived(r.len_recv, r.swap_s.at[3], r.swap_r.at[3], me)
+    for dx, n in ((3, 2), (1, 0), (3, 3), (1, 1), (2, 0), (2, 2), (2, 1), (2, 3)):
+        take(dx, n)
+    arrived(r.len_recv, r.swap_s.at[5], r.swap_r.at[5], me)
     r.lens[...] = jnp.where(me.moved, r.len_recv[...], r.len_send[...])
     for d in range(1, 4):
         shi, slo = me.along_y(4 - d)
@@ -471,11 +461,19 @@
     def _(i):
         project(r, k * 4 + i)
 
+    for d in range(1, 4):
+        shi, slo = me.along_y(4 - d)
+        arrived(r.wout.at[x % 2, :, :, slo, k, shi], r.yo_s.at[d - 1], r.yo_r.at[d - 1], me)
+    for n, to in ((0, right), (1, left)):
+        part = r.wout.at[x % 2, n, :, :, k]
+        sends.push(part, part, r.xq_s.at[n], r.xq_r.at[n], to)
+    part = r.wout.at[x % 2, :, :, :, k]
+    sends.push(part, part, r.core_s.at[2], r.core_r.at[2], me.sibling())
     for dx in range(4):
-        for half in range(2):
+        for n in range(4):
             arrived(
-                r.normed.at[(1 - k) * 4 + (x + dx) % 4, pl.ds(half * 128, 128)],
-                r.fw_s.at[dx, half], r.ag_r.at[4 + dx, half], me,
+                r.normed.at[(1 - k) * 4 + (x + dx) % 4, pl.ds(n * 64, 64)],
+                r.fw_s.at[dx, n], r.ag_r.at[4 + dx, n], me,
             )
 
     @pl.loop(0, 4)
@@ -485,12 +483,12 @@
     for i in range(4):
         attend(r, i, i)
 
-    for d in range(1, 4):
-        part = r.wout.at[(x + 4 - d) % 4, :, :, k]
-        arrived(part, r.xq_s.at[d - 1], r.xq_r.at[d - 1], me)
-        sends.push(part, part, r.core_s.at[d], r.core_r.at[d], me.sibling())
-
-    @pl.loop(4, 8)
+    for n in range(2):
+        part = r.wout.at[(x + 1) % 2, n, :, :, k]
+        arrived(part, r.xq_s.at[n], r.xq_r.at[n], me)
+        sends.push(part, part, r.core_s.at[n], r.core_r.at[n], me.sibling())
+
+    @pl.loop(4, 6)
     def _(i):
         attend(r, i, 4)
 
@@ -502,23 +500,30 @@
     def _():
         load_cot.wait()
 
-    for d in range(4):
-        arrived(r.wout.at[(x + 4 - d) % 4, :, :, 1 - k], r.core_s.at[d], r.core_r.at[d], me)
-
-    @pl.loop(0, 4)
-    def _(i):
+    arrived(r.wout.at[x % 2, :, :, :, 1 - k], r.core_s.at[2], r.core_r.at[2], me)
+    for n in range(2):
+        arrived(r.wout.at[(x + 1) % 2, n, :, :, 1 - k], r.core_s.at[n], r.core_r.at[n], me)
+    for dx in (2, 1, 3, 0):
+        px = (x + dx) % 4
         pair = jnp.zeros((ROWS, 256), F32)
         for q in range(4):
-            pair = pair + dot(r.cotr[:, q * 256 : (q + 1) * 256], r.wout[q, pl.ds(2 * i, 2)].reshape(256, 256), ABT)
-        r.dsend[2 * i] = pair[:, :HD].astype(BF16)
-        r.dsend[2 * i + 1] = pair[:, HD:].astype(BF16)
-
+            columns = r.wout[q % 2, q // 2, pl.ds(2 * px, 2)].reshape(256, 256)
+            pair = pair + dot(r.cotr[:, q * 256 : (q + 1) * 256], columns, ABT)
+        r.dsend[2 * px] = pair[:, :HD].astype(BF16)
+        r.dsend[2 * px + 1] = pair[:, HD:].astype(BF16)
+        for dk in range(2):
+            d = 4 * dk + dx
+            if d:
+                pk = (k + dk) % 2
+                sends.push(
+                    r.dsend.at[2 * px + pk], r.dmix.at[w], r.dm_s.at[d - 1], r.dm_r.at[d - 1], me.device(k=pk, x=px)
+                )
     r.dmix[w] = r.dsend[me.head]
-    for d in range(1, 8):
-        pk, px = me.row(d // 4, d % 4)
-        sends.push(
-            r.dsend.at[2 * px + pk], r.dmix.at[w], r.dm_s.at[d - 1], r.dm_r.at[d - 1], me.device(k=pk, x=px)
-        )
+
+    @pl.loop(6, 8)
+    def _(i):
+        attend(r, i, 4)
+
     for d in range(1, 8):
         sk, sx = row_source(d)
         arrived(r.dmix.at[sk * 4 + sx], r.dm_s.at[d - 1], r.dm_r.at[d - 1], me)
@@ -550,7 +555,7 @@
             r.msend.at[pk * 4 + px], r.mixed.at[me.head], r.mx_s.at[d - 1], r.mx_r.at[d - 1], me.device(k=pk, x=px)
         )
 
-    @pl.loop(0, 3)
+    @pl.loop(0, 4)
     def _(j):
         attend_back(r, j, 4)
 
@@ -563,14 +568,14 @@
         pair = jnp.concatenate([r.mixed[2 * n], r.mixed[2 * n + 1]], axis=1)
         product = dot(pair, r.cotr[...], ATB).astype(BF16)
         for q in range(4):
-            r.ps[q, pl.ds(2 * n, 2)] = product[:, q * 256 : (q + 1) * 256].reshape(2, 2, 2, 2, 16, 256)
-
-    sends.push(r.ps.at[:, :, :, 1 - k], r.pc, r.pc_s.at[0], r.pc_r.at[0], me.sibling())
+            r.ps[q % 2, q // 2, pl.ds(2 * n, 2)] = product[:, q * 256 : (q + 1) * 256].reshape(2, 2, 2, 2, 16, 256)
+
+    sends.push(r.ps.at[:, :, :, :, 1 - k], r.pc, r.pc_s.at[0], r.pc_r.at[0], me.sibling())
 
     joined = jnp.concatenate([r.mixed[h] for h in range(HEADS)], axis=1)
     for n in range(4):
         cols = pl.ds(n * 256, 256)
-        product = dot(joined, r.wout[n].reshape(D, 256))
+        product = dot(joined, r.wout[n % 2, n // 2].reshape(D, 256))
         r.lay[:, cols] = (product + r.tokr[:, cols].astype(F32)).astype(BF16)
     swap_lay = copy(r.lay, layer_out, r.sw_s.at[0], r.sw_r.at[0], me.partner())
     swap_grad = [
@@ -582,26 +587,23 @@
     def _():
         layer_out[...] = r.lay[...]
 
+    @pl.when(me.moved)
+    def _():
+        swap_lay.start()
+
+    attend_back(r, 4, 3)
     arrived(r.pc, r.pc_s.at[0], r.pc_r.at[0], me)
 
     @pl.loop(0, NZ)
     def _(n):
         for q in range(4):
-            r.pk_sum[q, n] = (r.ps[q, n, :, k].astype(F32) + r.pc[q, n].astype(F32)).astype(BF16)
-
-    for d in range(1, 4):
-        pk, px = me.row(0, d)
-        sends.push(r.pk_sum.at[px], r.pq.at[d - 1], r.pq_s.at[d - 1], r.pq_r.at[d - 1], me.device(x=px))
-
-    @pl.when(me.moved)
-    def _():
-        swap_lay.start()
-
-    @pl.loop(3, 4)
-    def _(j):
-        attend_back(r, j, 4)
-
-    for j in range(4, 8):
+            c, m = q % 2, q // 2
+            r.pk_sum[c, m, n] = (r.ps[c, m, n, :, k].astype(F32) + r.pc[c, m, n].astype(F32)).astype(BF16)
+
+    for n, to in ((0, right), (1, left)):
+        sends.push(r.pk_sum.at[(x + 1) % 2, n], r.pq.at[n], r.pq_s.at[n], r.pq_r.at[n], to)
+
+    for j in range(5, 8):
         attend_back(r, j, 7 - j)
 
     @pl.loop(0, 8)
@@ -648,6 +650,20 @@
     r.x2_send[...] = (r.esum[2] + r.es_recv[2].astype(F32)).astype(BF16)
     sends.push(r.x2_send.at[pl.ds(0, 128)], r.rl_recv.at[0], r.rl_s.at[0], r.rl_r.at[0], right)
     sends.push(r.x2_send.at[pl.ds(128, 128)], r.rl_recv.at[1], r.rl_s.at[1], r.rl_r.at[1], left)
+    for m in range(2):
+        arrived(r.pq.at[m], r.pq_s.at[m], r.pq_r.at[m], me)
+
+    @pl.loop(0, NZ)
+    def _(n):
+        for m in range(2):
+            r.pq_sum[m, n] = (r.pk_sum[x % 2, m, n].astype(F32) + r.pq[m, n].astype(F32)).astype(BF16)
+
+    for d in range(1, 4):
+        phi, plo = me.along_y(d)
+        sends.push(
+            r.pq_sum.at[:, :, plo, phi], r.py.at[d - 1], r.py_s.at[d - 1], r.py_r.at[d - 1], me.device(ylo=plo, yhi=phi)
+        )
+
     partial(3)
     from_sibling(1)
     to_neighbour(0, 1, None)
@@ -669,25 +685,24 @@
             r.gs.at[:, plo, 0, phi], r.gy.at[d - 1], r.gy_s.at[d - 1], r.gy_r.at[d - 1], me.device(ylo=plo, yhi=phi)
         )
 
-    for d in range(1, 4):
-        arrived(r.pq.at[d - 1], r.pq_s.at[d - 1], r.pq_r.at[d - 1], me)
-
-    @pl.loop(0, NZ)
-    def _(n):
-        total = r.pk_sum[x, n].astype(F32)
-        for d in range(3):
-            total = total + r.pq[d, n].astype(F32)
-        r.pq_sum[n] = total.astype(BF16)
-
-    for d in range(1, 4):
-        phi, plo = me.along_y(d)
-        sends.push(
-            r.pq_sum.at[:, plo, phi], r.py.at[d - 1], r.py_s.at[d - 1], r.py_r.at[d - 1], me.device(ylo=plo, yhi=phi)
-        )
-
     for side in range(2):
         arrived(r.rl_recv.at[side], r.rl_s.at[side], r.rl_r.at[side], me)
         to_neighbour(side, side, r.rl_recv[side])
+    for d in range(1, 4):
+        arrived(r.py.at[d - 1], r.py_s.at[d - 1], r.py_r.at[d - 1], me)
+
+    @pl.loop(0, NZ)
+    def _(n):
+        for m in range(2):
+            total = r.pq_sum[m, n, ylo, yhi].astype(F32)
+            for d in range(3):
+                total = total + r.py[d, m, n].astype(F32)
+            r.pz_send[n, m] = total.astype(BF16)
+
+    for d in range(1, NZ):
+        to = me.along_z(d)
+        sends.push(r.pz_send.at[to], r.pz.at[d - 1], r.pz_s.at[d - 1], r.pz_r.at[d - 1], me.device(z=to))
+
     partial(0)
 
     for d in range(1, 4):
@@ -703,33 +718,6 @@
     for d in range(1, NZ):
         to = me.along_z(d)
         sends.push(r.gz_send.at[to], r.gz.at[d - 1], r.gz_s.at[d - 1], r.gz_r.at[d - 1], me.device(z=to))
-    for d in range(1, NZ):
-        arrived(r.hz.at[d - 1], r.hz_s.at[d - 1], r.hz_r.at[d - 1], me)
-    for n in range(2):
-        total = r.gs[z, n, 1].astype(F32)
-        for d in range(7):
-            total = total + r.hz[d, n].astype(F32)
-        r.hy_send[n] = total.astype(BF16)
-    for d in range(1, 4):
-        phi, plo = me.along_y(d)
-        sends.push(
-            r.hy_send.at[plo, phi], r.hy.at[d - 1], r.hy_s.at[d - 1], r.hy_r.at[d - 1], me.device(ylo=plo, yhi=phi)
-        )
-
-    for d in range(1, 4):
-        arrived(r.py.at[d - 1], r.py_s.at[d - 1], r.py_r.at[d - 1], me)
-
-    @pl.loop(0, NZ)
-    def _(n):
-        total = r.pq_sum[n, ylo, yhi].astype(F32)
-        for d in range(3):
-            total = total + r.py[d, n].astype(F32)
-        r.pz_send[n] = total.astype(BF16)
-
-    for d in range(1, NZ):
-        to = me.along_z(d)
-        sends.push(r.pz_send.at[to], r.pz.at[d - 1], r.pz_s.at[d - 1], r.pz_r.at[d - 1], me.device(z=to))
-
     from_sibling(0)
 
     def finish(half):
@@ -761,13 +749,26 @@
     finish(1)
 
     for d in range(1, NZ):
+        arrived(r.hz.at[d - 1], r.hz_s.at[d - 1], r.hz_r.at[d - 1], me)
+    for n in range(2):
+        total = r.gs[z, n, 1].astype(F32)
+        for d in range(7):
+            total = total + r.hz[d, n].astype(F32)
+        r.hy_send[n] = total.astype(BF16)
+    for d in range(1, 4):
+        phi, plo = me.along_y(d)
+        sends.push(
+            r.hy_send.at[plo, phi], r.hy.at[d - 1], r.hy_s.at[d - 1], r.hy_r.at[d - 1], me.device(ylo=plo, yhi=phi)
+        )
+
+    for d in range(1, NZ):
         arrived(r.pz.at[d - 1], r.pz_s.at[d - 1], r.pz_r.at[d - 1], me)
     total = r.pz_send[z].astype(F32)
     for d in range(1, NZ):
         total = total + r.pz[d - 1].astype(F32)
     for px in range(4):
-        for b in range(2):
-            r.px_f[px, b * 4 : b * 4 + 4, :] = total[px * 4 : px * 4 + 4, b * HD : (b + 1) * HD]
+        for b in range(4):
+            r.px_f[px, b * 4 : b * 4 + 4, :] = total[b // 2, px * 4 : px * 4 + 4, b % 2 * HD : (b % 2 + 1) * HD]
     r.px_recv[x] = r.px_f[x]
     for d in range(1, 4):
         pk, px = me.row(0, d)
@@ -798,8 +799,11 @@
 
     for d in range(1, 4):
         arrived(r.px_recv.at[(x + 4 - d) % 4], r.px_s.at[d - 1], r.px_r.at[d - 1], me)
-    for b in range(8):
-        wo_grad[:, b * HD : (b + 1) * HD] = r.px_recv[b // 2, (b % 2) * 4 : (b % 2) * 4 + 4]
+    for c in range(2):
+        total = r.px_recv[c] + r.px_recv[c + 2]
+        for n in range(4):
+            b = n // 2 * 4 + c * 2 + n % 2
+            wo_grad[:, b * HD : (b + 1) * HD] = total[n * 4 : n * 4 + 4]
     for d in range(1, 8):
         sk, sx = row_source(d)
         arrived(r.gx_recv.at[sk * 4 + sx], r.gx_s.at[d - 1], r.gx_r.at[d - 1], me)
@@ -808,7 +812,7 @@
         for b in range(4):
             wi_grad[:, b * D + h * HD : b * D + (h + 1) * HD] = r.gx_recv[src, b * 4 : b * 4 + 4, :]
     sends.drain()
-    for one in own_sends + first_sends:
+    for one in to_right + to_left + to_sibling + list(relay.values()) + list(relay_sibling.values()):
         one.wait_send()
 
     @pl.when(me.moved)

time: 130 us -> 125 us (0.962)
  Pallas kernels: 125 us -> 120 us
    pallas_call x1, Pallas kernels: 125 us -> 120 us  [local(): pl.pallas_call(kernel, out_shape=[jax.ShapeDtypeStruct(s, t) for s, t in...]
where the time goes in v4:
time: 125 us
  Pallas kernels  120 us (96%)
  local copies, waits for them, and re-layouts  4.11 us (3%)
    pallas_call x1, Pallas kernels, local(): pl.pallas_call(kernel, out_shape=[jax.ShapeDtypeStruct(s, t) for s, t in...  120 us
    unnamed x10, local copies, waits for them, and re-layouts  4.11 us

profile of v4, /device:TPU:1, one launch (start us, length us, event | category | flops | bytes accessed | tf_op | source)
XLA Modules:
  0.0 125.0 jit_solution(10266447326111217060)
XLA Ops:
  0.6 120.2 %layer.1 = (bf16[256,1024]{1,0:T(8,128)(2,1)}, bf16[256,1024]{1,0:T(8,128)(2,1)}, f32[4,4096]{1,0:T(4,128)}, f32[4,1024]{1,0:T(4,128)}) custom-call(bf16[256,1024]{1,0:T(8,128)(2,1)} %tok.1, bf16[256,1024]{1,0:T(8,128)(2,1)} %cot.1, bf16[4,4096]{1,0:T(4,128)(2,1)} %wi.1, bf16[4,1024]{1,0:T(4,128)(2,1)} %wo.1, s32[1,4]{1,0:T(1,128)} %lengths.1), custom_call_target="tpu_custom_call" | custom-call | tf_op jit(solution)/shard_map/layer/pallas_call | solution.py:835
  120.9 0.0 copy-start
  120.9 1.9 %copy.13 = bf16[256,1024]{1,0:T(8,128)(2,1)} copy(bf16[256,1024]{1,0:T(8,128)(2,1)} %get-tuple-element.8) | data formatting | bytes 1048576
  122.8 0.0 copy-done
  122.8 0.0 copy-start.1
  122.8 0.8 copy.14
  123.6 0.1 copy-done.1
  123.7 0.0 copy-start.2
  123.7 0.6 copy.15
  124.3 0.1 copy-done.2
  124.4 0.6 copy.16
Async XLA Ops:
  120.9 1.9 %copy-start = (bf16[256,1024]{1,0:T(8,128)(2,1)S(1)}, bf16[256,1024]{1,0:T(8,128)(2,1)}, u32[]{:S(2)}) copy-start(bf16[256,1024]{1,0:T(8,128)(2,1)} %get-tuple-element.9) | copy-start | bytes 1572868
  122.8 0.9 copy-start.1
  123.7 0.7 copy-start.2

commit v5 on v4

--- a/solution.py
+++ b/solution.py
@@ -140,7 +140,9 @@
     "win": ((NZ, 2, 2, 2, 16, 512), BF16), "wout": ((2, 2, NZ, 2, 2, 2, 16, 256), BF16),
     "normed": ((8, ROWS, D), BF16), "gated": ((8, ROWS, 512), BF16), "slope": ((8, ROWS, 512), BF16),
     "dsend": ((8, ROWS, HD), BF16), "dmix": ((8, ROWS, HD), BF16),
-    "attn": ((8, ROWS, HD), BF16), "stats": ((4, 8, ROWS), F32), "every": ((8, 4, 8, ROWS), F32),
+    "attn": ((8, ROWS, HD), BF16), "centre": ((8, ROWS, HD), F32), "dpart": ((4, ROWS, 256), F32),
+    "stats_a": ((2, 8, ROWS), F32), "every_a": ((8, 2, 8, ROWS), F32),
+    "stats_b": ((2, 8, ROWS), F32), "every_b": ((8, 2, 8, ROWS), F32),
     "comb": ((128, ROWS), F32), "msend": ((8, ROWS, HD), BF16), "mixed": ((8, ROWS, HD), BF16),
     "dattn": ((8, ROWS, HD), BF16), "dhidden": ((8, ROWS, 512), BF16), "dquery": ((8, ROWS, HD), F32),
     "lay": ((ROWS, D), BF16), "grad": ((ROWS, D), BF16),
@@ -160,7 +162,7 @@
 SEMAPHORES = {
     "load": (2,), "swap": (6,), "xi": (7,), "xo": (3,), "zi": (7,), "zo": (7,), "yi": (3,), "yo": (3,), "xq": (2,), "core": (3,),
     "zj": (7,), "yj": (3,),
-    "ag": (8, 4), "fw": (4, 4), "dm": (7,), "st": (7,), "mx": (7,), "sib": (4,), "rl": (2,), "nb": (2, 2),
+    "ag": (8, 4), "fw": (4, 4), "dm": (7,), "sa": (7,), "sb": (7,), "mx": (7,), "sib": (4,), "rl": (2,), "nb": (2, 2),
     "gy": (3,), "gz": (7,), "hy": (3,), "hz": (7,), "gx": (7,),
     "pc": (1,), "pq": (2,), "py": (3,), "pz": (7,), "px": (3,), "sw": (3,),
 }
@@ -204,28 +206,32 @@
     r.attn[i] = total.astype(BF16)
 
 
-def row_stats(r, pair, side):
-    i = 2 * pair + side
+def two_columns(first, second):
+    lane = lax.broadcasted_iota(jnp.int32, (ROWS, HD), 1)
+    return jnp.where(lane == 0, first, jnp.where(lane == 1, second, 0.0)).T[0:2]
+
+
+def attn_stats(r, quad, n):
+    i = 4 * quad + n
     value = r.attn[i].astype(F32)
-    upstream = r.dmix[i].astype(F32) * r.gated[i, :, 0:128].astype(F32)
     mean = jnp.mean(value, axis=-1, keepdims=True)
     centre = value - mean
-    parts = (
-        mean,
-        jnp.sum(centre * centre, axis=-1, keepdims=True),
-        jnp.sum(upstream, axis=-1, keepdims=True),
-        jnp.sum(upstream * centre, axis=-1, keepdims=True),
+    r.centre[i] = centre
+    r.stats_a[quad, 2 * n : 2 * n + 2] = two_columns(mean, jnp.sum(centre * centre, axis=-1, keepdims=True))
+
+
+def upstream_stats(r, quad, n):
+    i = 4 * quad + n
+    upstream = r.dmix[i].astype(F32) * r.gated[i, :, 0:128].astype(F32)
+    r.stats_b[quad, 2 * n : 2 * n + 2] = two_columns(
+        jnp.sum(upstream, axis=-1, keepdims=True), jnp.sum(upstream * r.centre[i], axis=-1, keepdims=True)
     )
-    lane = lax.broadcasted_iota(jnp.int32, (ROWS, HD), 1)
-    packed = jnp.zeros((ROWS, HD), F32)
-    for n, part in enumerate(parts):
-        packed = jnp.where(lane == n, part, packed)
-    r.stats[pair, 4 * side : 4 * side + 4] = packed.T[0:4]
-
-
-def gate_rows(r, pair, side):
-    i = 2 * pair + side
-    mean, second, total, cross = (r.every[:, pair, 4 * side + n, :] for n in range(4))
+
+
+def gate_rows(r, quad, n):
+    i = 4 * quad + n
+    mean, second = (r.every_a[:, quad, 2 * n + m, :] for m in range(2))
+    total, cross = (r.every_b[:, quad, 2 * n + m, :] for m in range(2))
     middle = jnp.mean(mean, axis=0, keepdims=True)
     apart = mean - middle
     variance = jnp.sum(second + HD * apart * apart, axis=0, keepdims=True) / D
@@ -483,6 +489,25 @@
     for i in range(4):
         attend(r, i, i)
 
+    @pl.when(me.moved)
+    def _():
+        swap_cot.wait_recv()
+
+    @pl.when(stays)
+    def _():
+        load_cot.wait()
+
+    arrived(r.wout.at[x % 2, :, :, :, 1 - k], r.core_s.at[2], r.core_r.at[2], me)
+    def through(px, side):
+        pair = jnp.zeros((ROWS, 256), F32)
+        for m in range(2):
+            cols = pl.ds(pl.multiple_of((side + 2 * m) * 256, 256), 256)
+            pair = pair + dot(r.cotr[:, cols], r.wout[side, m, pl.ds(2 * px, 2)].reshape(256, 256), ABT)
+        return pair
+
+    for dx in range(4):
+        r.dpart[dx] = through((x + dx) % 4, x % 2)
+
     for n in range(2):
         part = r.wout.at[(x + 1) % 2, n, :, :, k]
         arrived(part, r.xq_s.at[n], r.xq_r.at[n], me)
@@ -492,23 +517,11 @@
     def _(i):
         attend(r, i, 4)
 
-    @pl.when(me.moved)
-    def _():
-        swap_cot.wait_recv()
-
-    @pl.when(stays)
-    def _():
-        load_cot.wait()
-
-    arrived(r.wout.at[x % 2, :, :, :, 1 - k], r.core_s.at[2], r.core_r.at[2], me)
     for n in range(2):
         arrived(r.wout.at[(x + 1) % 2, n, :, :, 1 - k], r.core_s.at[n], r.core_r.at[n], me)
     for dx in (2, 1, 3, 0):
         px = (x + dx) % 4
-        pair = jnp.zeros((ROWS, 256), F32)
-        for q in range(4):
-            columns = r.wout[q % 2, q // 2, pl.ds(2 * px, 2)].reshape(256, 256)
-            pair = pair + dot(r.cotr[:, q * 256 : (q + 1) * 256], columns, ABT)
+        pair = r.dpart[dx] + through(px, (x + 1) % 2)
         r.dsend[2 * px] = pair[:, :HD].astype(BF16)
         r.dsend[2 * px + 1] = pair[:, HD:].astype(BF16)
         for dk in range(2):
@@ -524,29 +537,41 @@
     def _(i):
         attend(r, i, 4)
 
+    @pl.loop(0, 2)
+    def _(quad):
+        for n in range(4):
+            attn_stats(r, quad, n)
+
+    for d in range(1, 8):
+        pk, px = me.row(d // 4, d % 4)
+        sends.push(r.stats_a, r.every_a.at[w], r.sa_s.at[d - 1], r.sa_r.at[d - 1], me.device(k=pk, x=px))
+    r.every_a[w] = r.stats_a[...]
+    r.comb[...] = jnp.zeros_like(r.comb)
+    r.dquery[...] = jnp.zeros_like(r.dquery)
     for d in range(1, 8):
         sk, sx = row_source(d)
         arrived(r.dmix.at[sk * 4 + sx], r.dm_s.at[d - 1], r.dm_r.at[d - 1], me)
 
-    @pl.loop(0, 4)
-    def _(pair):
-        row_stats(r, pair, 0)
-        row_stats(r, pair, 1)
+    @pl.loop(0, 2)
+    def _(quad):
+        for n in range(4):
+            upstream_stats(r, quad, n)
 
     for d in range(1, 8):
         pk, px = me.row(d // 4, d % 4)
-        sends.push(r.stats, r.every.at[w], r.st_s.at[d - 1], r.st_r.at[d - 1], me.device(k=pk, x=px))
-    r.every[w] = r.stats[...]
-    r.comb[...] = jnp.zeros_like(r.comb)
-    r.dquery[...] = jnp.zeros_like(r.dquery)
+        sends.push(r.stats_b, r.every_b.at[w], r.sb_s.at[d - 1], r.sb_r.at[d - 1], me.device(k=pk, x=px))
+    r.every_b[w] = r.stats_b[...]
     for d in range(1, 8):
         sk, sx = row_source(d)
-        arrived(r.every.at[sk * 4 + sx], r.st_s.at[d - 1], r.st_r.at[d - 1], me)
-
-    @pl.loop(0, 4)
-    def _(pair):
-        gate_rows(r, pair, 0)
-        gate_rows(r, pair, 1)
+        arrived(r.every_a.at[sk * 4 + sx], r.sa_s.at[d - 1], r.sa_r.at[d - 1], me)
+    for d in range(1, 8):
+        sk, sx = row_source(d)
+        arrived(r.every_b.at[sk * 4 + sx], r.sb_s.at[d - 1], r.sb_r.at[d - 1], me)
+
+    @pl.loop(0, 2)
+    def _(quad):
+        for n in range(4):
+            gate_rows(r, quad, n)
 
     r.mixed[me.head] = r.msend[w]
     for d in range(1, 8):

time: 125 us -> 122 us (0.976)
  Pallas kernels: 120 us -> 117 us
    pallas_call x1, Pallas kernels: 120 us -> 117 us  [local(): pl.pallas_call(kernel, out_shape=[jax.ShapeDtypeStruct(s, t) for s, t in...]
where the time goes in v5:
time: 122 us
  Pallas kernels  117 us (96%)
  local copies, waits for them, and re-layouts  4.11 us (3%)
    pallas_call x1, Pallas kernels, local(): pl.pallas_call(kernel, out_shape=[jax.ShapeDtypeStruct(s, t) for s, t in...  117 us
    unnamed x10, local copies, waits for them, and re-layouts  4.11 us

profile of v5, /device:TPU:1, one launch (start us, length us, event | category | flops | bytes accessed | tf_op | source)
XLA Modules:
  0.0 122.0 jit_solution(18256464766155369147)
XLA Ops:
  0.6 117.2 %layer.1 = (bf16[256,1024]{1,0:T(8,128)(2,1)}, bf16[256,1024]{1,0:T(8,128)(2,1)}, f32[4,4096]{1,0:T(4,128)}, f32[4,1024]{1,0:T(4,128)}) custom-call(bf16[256,1024]{1,0:T(8,128)(2,1)} %tok.1, bf16[256,1024]{1,0:T(8,128)(2,1)} %cot.1, bf16[4,4096]{1,0:T(4,128)(2,1)} %wi.1, bf16[4,1024]{1,0:T(4,128)(2,1)} %wo.1, s32[1,4]{1,0:T(1,128)} %lengths.1), custom_call_target="tpu_custom_call" | custom-call | tf_op jit(solution)/shard_map/layer/pallas_call | solution.py:860
  117.8 0.0 copy-start
  117.8 1.9 %copy.13 = bf16[256,1024]{1,0:T(8,128)(2,1)} copy(bf16[256,1024]{1,0:T(8,128)(2,1)} %get-tuple-element.8) | data formatting | bytes 1048576
  119.8 0.0 copy-done
  119.8 0.0 copy-start.1
  119.8 0.8 copy.14
  120.6 0.1 copy-done.1
  120.6 0.0 copy-start.2
  120.6 0.6 copy.15
  121.3 0.1 copy-done.2
  121.3 0.6 copy.16
Async XLA Ops:
  117.8 1.9 %copy-start = (bf16[256,1024]{1,0:T(8,128)(2,1)S(1)}, bf16[256,1024]{1,0:T(8,128)(2,1)}, u32[]{:S(2)}) copy-start(bf16[256,1024]{1,0:T(8,128)(2,1)} %get-tuple-element.9) | copy-start | bytes 1572868
  119.8 0.9 copy-start.1
  120.6 0.7 copy-start.2

commit v6 on v5

--- a/solution.py
+++ b/solution.py
@@ -850,16 +850,25 @@
             one.wait()
 
 
+def hand_on(*refs):
+    copies = [pltpu.make_async_copy(refs[n], refs[4 + n], refs[8].at[n]) for n in range(4)]
+    for one in copies:
+        one.start()
+    for one in copies:
+        one.wait()
+
+
 def local(tokens, lengths, in_weight, out_weight, cotangent):
     anywhere = pl.BlockSpec(memory_space=pl.ANY)
     shapes = [((ROWS, D), BF16), ((ROWS, D), BF16), ((4, 4 * D), F32), ((4, D), F32)]
     scratch = [pltpu.VMEM(shape, kind) for shape, kind in BUFFERS.values()]
     for shape in SEMAPHORES.values():
         scratch += [DMA(shape), DMA(shape)]
-    return tuple(
+    shapes = [jax.ShapeDtypeStruct(s, t) for s, t in shapes]
+    results = (
         pl.pallas_call(
             kernel,
-            out_shape=[jax.ShapeDtypeStruct(s, t) for s, t in shapes],
+            out_shape=shapes,
             in_specs=[anywhere, anywhere, VMEM, VMEM, VMEM],
             out_specs=[VMEM] * 4,
             scratch_shapes=scratch,
@@ -869,6 +878,16 @@
             name="layer",
         )(tokens, cotangent, in_weight, out_weight, lengths)
     )
+    return tuple(
+        pl.pallas_call(
+            hand_on,
+            out_shape=shapes,
+            in_specs=[VMEM] * 4,
+            out_specs=[anywhere] * 4,
+            scratch_shapes=[DMA((4,))],
+            name="hand_on",
+        )(*results)
+    )
 
 
 def solution(mesh):

time: 122 us -> 120 us (0.984)
  local copies, waits for them, and re-layouts: 4.11 us -> 0 us
  Pallas kernels: 117 us -> 119 us
    unnamed x10 -> x0, local copies, waits for them, and re-layouts: 4.11 us -> none
    pallas_call x1 -> x2, Pallas kernels: 117 us -> 119 us  [the longest x1 117 us: local(): pl.pallas_call(kernel, out_shape=shapes, in_specs=[anywhere, anywhere, VM...]
where the time goes in v6:
time: 120 us
  Pallas kernels  119 us (99%)
    pallas_call x1, Pallas kernels, local(): pl.pallas_call(kernel, out_shape=shapes, in_specs=[anywhere, anywhere, VM...  117 us

profile of v6, /device:TPU:1, one launch (start us, length us, event | category | flops | bytes accessed | tf_op | source)
XLA Modules:
  0.0 120.2 jit_solution(2698681491786460859)
XLA Ops:
  0.6 117.2 %layer.1 = (bf16[256,1024]{1,0:T(8,128)(2,1)}, bf16[256,1024]{1,0:T(8,128)(2,1)}, f32[4,4096]{1,0:T(4,128)}, f32[4,1024]{1,0:T(4,128)}) custom-call(bf16[256,1024]{1,0:T(8,128)(2,1)} %tok.1, bf16[256,1024]{1,0:T(8,128)(2,1)} %cot.1, bf16[4,4096]{1,0:T(4,128)(2,1)} %wi.1, bf16[4,1024]{1,0:T(4,128)(2,1)} %wo.1, s32[1,4]{1,0:T(1,128)} %lengths.1), custom_call_target="tpu_custom_call" | custom-call | tf_op jit(solution)/shard_map/layer/pallas_call | solution.py:869
  117.8 2.2 %hand_on.1 = (bf16[256,1024]{1,0:T(8,128)(2,1)}, bf16[256,1024]{1,0:T(8,128)(2,1)}, f32[4,4096]{1,0:T(4,128)}, f32[4,1024]{1,0:T(4,128)}) custom-call(bf16[256,1024]{1,0:T(8,128)(2,1)} %get-tuple-element.8.refs_0_, bf16[256,1024]{1,0:T(8,128)(2,1)} %get-tuple-element.9.refs_1_, f32[4,4096]{1,0:T(4,128)} %get-tuple-element.10.refs_2_, ...), custom_call_target="tpu_custom_call" | custom-call | tf_op jit(solution)/shard_map/hand_on/pallas_call | solution.py:882
